TPU v7x, 256 devices: a whole 4x4x8 slice. The times are simulated.
256 devices in a mesh: row: 32 (over z_lo, y, x), col: 8 (over z_hi, core).
Axes of the slice: x: 4, y: 4, z: 8 (z_hi: 4, z_lo: 2; z = z_hi * 2 + z_lo), core: 2. Of those that a mesh axis runs over, the one named last changes fastest.
Arguments:
- features: bfloat16 [131072, 128], P(('col', 'row')), may hold values from -6 to 6
- weight: bfloat16 [128, 128], replicated, may hold values from -0.5 to 0.5
- cotangent: bfloat16 [131072, 128], P(('row', 'col')), may hold values from -6 to 6
- tile_values: bfloat16 [32, 8, 128, 128, 128], P('row', 'col'), may hold values from -0.09375 to 0.09375
- tile_coords: int32 [32, 8, 128, 2], P('row', 'col'), may hold values from 0 to 127, as said below
- tile_count: int32 [32, 8], P('row', 'col'), may hold values from 64 to 128, as said below
- row_degree: int32 [131072], P(('row', 'col')), may hold values from 1 to 8
- col_degree: int32 [131072], P(('col', 'row')), may hold values from 1 to 8
Outputs:
- layer_out: bfloat16 [131072, 128], P(('row', 'col'))
- grad_input: bfloat16 [131072, 128], P(('col', 'row'))
- grad_weight: float32 [128, 128], replicated
Inputs may be any that keep to these rules, and one draw needn't show every extreme that they name: `tile_coords`: entry 0 is a tile row below 32, entry 1 a tile column below 128; padding slots hold coordinates too. A coordinate pair may repeat within a block; such tiles add. `tile_count`: slots at or beyond the count are padding whose values are not part of the matrix. At least half of a block's slots are live, and some block has all 128 live.
All inputs are finite; a program needn't handle non-finite values.
Results may differ from a plain program's by a relative error of at most 0.0054.
Values may be sent and summed in bfloat16 or wider, within the bound.
A program may use at most 64 MiB of HBM per device.

v0:
```python
import jax
import jax.numpy as jnp
from jax import lax
from jax.sharding import PartitionSpec as P


def tile_products(values, coords, weights, rows_in, pick_dim, transpose):
    tile = values.shape[1]
    width = rows_in.shape[1]
    in_tiles = rows_in.reshape(rows_in.shape[0] // tile, tile, width)
    picked = in_tiles[coords[:, pick_dim]]
    if transpose:
        prods = jnp.einsum("tji,tjf->tif", values, picked, preferred_element_type=jnp.float32)
    else:
        prods = jnp.einsum("tij,tjf->tif", values, picked, preferred_element_type=jnp.float32)
    return prods * weights[:, None, None]


def place_tiles(prods, targets, first, out_tiles):
    tile = prods.shape[1]
    width = prods.shape[2]
    relative = targets - first
    inside = jnp.logical_and(relative >= 0, relative < out_tiles)
    places = jnp.where(inside, relative, out_tiles)
    summed = jnp.zeros((out_tiles, tile, width), jnp.float32).at[places].add(prods, mode="drop")
    return summed.reshape(out_tiles * tile, width)


def body(features, weight, cotangent, tile_values, tile_coords, tile_count, row_degree, col_degree):
    values = tile_values[0, 0]
    coords = tile_coords[0, 0]
    count = tile_count[0, 0]
    tile = values.shape[1]
    nodes = features.shape[0]
    row_tiles = nodes * lax.axis_size("col") // tile
    col_tiles = nodes * lax.axis_size("row") // tile
    row_scale = 1.0 / jnp.sqrt(row_degree.astype(jnp.float32))
    col_scale = 1.0 / jnp.sqrt(col_degree.astype(jnp.float32))
    live = (jnp.arange(values.shape[0]) < count).astype(jnp.float32)
    scaled_in = (features.astype(jnp.float32) * col_scale[:, None]).astype(jnp.bfloat16)
    gathered = lax.all_gather(scaled_in, "row", axis=0, tiled=True)
    forward_prods = tile_products(values, coords, live, gathered, 1, False)
    partial_rows = place_tiles(forward_prods, coords[:, 0], 0, row_tiles)
    summed = lax.psum_scatter(partial_rows, "col", scatter_dimension=0, tiled=True)
    hidden = (row_scale[:, None] * summed).astype(jnp.bfloat16)
    layer_out = jnp.dot(hidden, weight, preferred_element_type=jnp.float32).astype(jnp.bfloat16)
    grad_hidden = lax.dot_general(
        cotangent, weight, (((1,), (1,)), ((), ())), preferred_element_type=jnp.float32
    )
    scaled_grad = (row_scale[:, None] * grad_hidden).astype(jnp.bfloat16)
    grad_rows = lax.all_gather(scaled_grad, "col", axis=0, tiled=True)
    back_prods = tile_products(values, coords, live, grad_rows, 0, True)
    partial_cols = place_tiles(back_prods, coords[:, 1], 0, col_tiles)
    back = lax.psum_scatter(partial_cols, "row", scatter_dimension=0, tiled=True)
    grad_input = (col_scale[:, None] * back).astype(jnp.bfloat16)
    local_grad = jnp.einsum("nf,ng->fg", hidden, cotangent, preferred_element_type=jnp.float32)
    grad_weight = lax.psum(local_grad, ("row", "col"))
    return (layer_out, grad_input, grad_weight)


def solution(mesh):
    in_specs = (
        P(("col", "row"), None),
        P(),
        P(("row", "col"), None),
        P("row", "col", None, None, None),
        P("row", "col", None, None),
        P("row", "col"),
        P(("row", "col")),
        P(("col", "row")),
    )
    out_specs = (P(("row", "col"), None), P(("col", "row"), None), P())
    return jax.shard_map(body, mesh=mesh, in_specs=in_specs, out_specs=out_specs, check_vma=False)
```

profile of v0, /device:TPU:1, one launch (start us, length us, event | category | flops | bytes accessed | tf_op | source)
XLA Modules:
  0.0 773.6 jit_solution(9236898124754253695)
XLA Ops:
  7.2 0.0 all-gather.5.cloned.1.call-start
  7.2 0.7 convert_rsqrt_fusion.1
  7.9 0.1 copy-done
  8.1 1.6 fusion.8
  9.7 0.0 all-gather.5.cloned.1.call-update
  9.7 0.0 reduce-scatter.5.cloned.1.call-start
  10.4 0.8 fusion.12
  11.2 33.5 %all-gather.5.cloned.1.call-done = bf16[4096,128]{1,0:T(8,128)(2,1)} async-done(((bf16[512,128]{1,0:T(8,128)(2,1)}), bf16[4096,128]{1,0:T(8,128)(2,1)}) %all-gather.5.cloned.1.call-update) | async-done | bytes 1048592 | tf_op jit(solution)/shard_map/all_gather | solution.py:51
  44.7 4.2 gather_fusion.1
  49.0 8.7 %multiply_bitcast_fusion = f32[128,128,128]{1,2,0:T(8,128)} fusion(f32[128]{0:T(128)S(1)} %compare_convert_fusion, bf16[128,128,128]{2,1,0:T(8,128)(2,1)} %gather_fusion.1, bf16[1,1,128,128,128]{4,3,2,1,0:T(8,128)(2,1)} %param.11), kind=kOutput, calls=%fused_computation.4 | convolution fusion | flops 538968064 | bytes 16777728 | tf_op jit(solution)/shard_map/tji,tjf->tif/dot_general | solution.py:13
  57.7 9.0 %copy.16 = f32[128,128,128]{2,1,0:T(8,128)} copy(f32[128,128,128]{1,2,0:T(8,128)} %multiply_bitcast_fusion) | data formatting | bytes 16777216 | tf_op jit(solution)/shard_map/mul | solution.py:16
  66.7 4.3 broadcast_in_dim.8
  71.0 26.5 %scatter_fusion.1 = f32[128,128,128]{2,1,0:T(8,128)} fusion(f32[128,128,128]{2,1,0:T(8,128)} %broadcast_in_dim.8, s32[128]{0:T(128)S(1)} %get-tuple-element.8, f32[128,128,128]{2,1,0:T(8,128)} %copy.16), kind=kCustom, calls=%fused_computation.3 | custom fusion | flops 2097152 | bytes 25166336 | tf_op jit(solution)/shard_map/scatter-add | solution.py:25
  97.5 0.0 reduce-scatter.5.cloned.1.call-update
  97.5 0.0 all-gather.3.cloned.1.call-start
  97.6 0.6 copy-done.4
  98.2 156.3 %reduce-scatter.5.cloned.1.call-done = f32[512,128]{1,0:T(8,128)} async-done(((f32[16384,128]{1,0:T(8,128)}), f32[512,128]{1,0:T(8,128)}) %reduce-scatter.5.cloned.1.call-update) | async-done | bytes 262160 | tf_op jit(solution)/shard_map/reduce_scatter | solution.py:54
  254.5 1.8 multiply_convert_fusion
  256.3 0.0 reduce-scatter.3.cloned.1.call-start
  256.4 159.5 %all-gather.3.cloned.1.call-done = bf16[16384,128]{1,0:T(8,128)(2,1)} async-done(((bf16[512,128]{1,0:T(8,128)(2,1)}), bf16[16384,128]{1,0:T(8,128)(2,1)}) %all-gather.3.cloned.1.call-update) | async-done | bytes 4194320 | tf_op jit(solution)/shard_map/all_gather | solution.py:41
  416.0 5.2 gather_fusion
  421.2 9.8 %multiply_bitcast_fusion.1 = f32[128,128,128]{1,2,0:T(8,128)} fusion(f32[128]{0:T(128)S(1)} %compare_convert_fusion, bf16[128,128,128]{2,1,0:T(8,128)(2,1)} %gather_fusion, bf16[1,1,128,128,128]{4,3,2,1,0:T(8,128)(2,1)} %param.11), kind=kOutput, calls=%fused_computation.5 | convolution fusion | flops 538968064 | bytes 16777728 | tf_op jit(solution)/shard_map/tij,tjf->tif/dot_general | solution.py:15
  431.0 9.0 %copy.14 = f32[128,128,128]{2,1,0:T(8,128)} copy(f32[128,128,128]{1,2,0:T(8,128)} %multiply_bitcast_fusion.1) | data formatting | bytes 16777216 | tf_op jit(solution)/shard_map/mul | solution.py:16
  440.0 0.2 broadcast_in_dim.7
  440.2 17.1 %scatter_fusion = f32[32,128,128]{2,1,0:T(8,128)S(1)} fusion(f32[32,128,128]{2,1,0:T(8,128)S(1)} %broadcast_in_dim.7, s32[128]{0:T(128)S(1)} %get-tuple-element.6, f32[128,128,128]{2,1,0:T(8,128)} %copy.14), kind=kCustom, calls=%fused_computation.2 | custom fusion | flops 2097152 | bytes 25166336 | tf_op jit(solution)/shard_map/scatter-add | solution.py:25
  457.3 1.3 copy-done.1
  458.6 0.0 all-reduce.2.cloned.1.call-start
  458.7 62.7 %reduce-scatter.3.cloned.1.call-done = f32[512,128]{1,0:T(8,128)} async-done(((f32[4096,128]{1,0:T(8,128)}), f32[512,128]{1,0:T(8,128)}) %reduce-scatter.3.cloned.1.call-update) | async-done | bytes 262160 | tf_op jit(solution)/shard_map/reduce_scatter | solution.py:44
  521.4 1.9 fusion.13
  523.3 1.9 convolution_convert_fusion
  525.2 240.4 %all-reduce.2.cloned.1.call-done = f32[128,128]{1,0:T(8,128)} async-done(((f32[128,128]{1,0:T(8,128)}), f32[128,128]{1,0:T(8,128)}) %all-reduce.2.cloned.1.call-update) | async-done | bytes 65552 | tf_op jit(solution)/shard_map/psum | solution.py:57
  765.6 1.5 copy.23
  (14 shorter events, 0.1 us)
Async XLA Ops:
  7.2 0.9 copy-start
  7.2 37.5 %all-gather.5.cloned.1.call-start = ((), (), s32[]{:S(2)}) async-start(), calls=%async_computation.4 | async-start | bytes 1179648 | tf_op jit(solution)/shard_map/all_gather | solution.py:51
  9.7 244.8 %reduce-scatter.5.cloned.1.call-start = ((), (), s32[]{:S(2)}) async-start(), calls=%async_computation.5 | async-start | bytes 8650752 | tf_op jit(solution)/shard_map/reduce_scatter | solution.py:54
  97.5 0.7 copy-start.4
  97.5 157.0 %copy-start.2 = (bf16[512,128]{1,0:T(8,128)(2,1)S(1)}, bf16[512,128]{1,0:T(8,128)(2,1)}, u32[]{:S(2)}) copy-start(bf16[512,128]{1,0:T(8,128)(2,1)} %param.8) | copy-start | bytes 393220
  97.5 318.4 %all-gather.3.cloned.1.call-start = ((), (), s32[]{:S(2)}) async-start(), calls=%async_computation.2 | async-start | bytes 4325376 | tf_op jit(solution)/shard_map/all_gather | solution.py:41
  256.3 265.1 %reduce-scatter.3.cloned.1.call-start = ((), (), s32[]{:S(2)}) async-start(), calls=%async_computation.3 | async-start | bytes 2359296 | tf_op jit(solution)/shard_map/reduce_scatter | solution.py:44
  440.2 83.1 %copy-start.3 = (bf16[128,128]{1,0:T(8,128)(2,1)S(1)}, bf16[128,128]{1,0:T(8,128)(2,1)}, u32[]{:S(2)}) copy-start(bf16[128,128]{1,0:T(8,128)(2,1)} %param.9) | copy-start | bytes 98308
  457.3 1.3 copy-start.1
  458.6 307.0 %all-reduce.2.cloned.1.call-start = ((), (), s32[]{:S(2)}) async-start(), calls=%async_computation.6 | async-start | bytes 131072 | tf_op jit(solution)/shard_map/psum | solution.py:57
Sparse Core Ops, SparseCore 0:
  10.4 34.2 all-gather.4
  97.7 156.8 reduce-scatter.4
  256.9 158.9 all-gather.2
  458.8 62.5 reduce-scatter.2
  527.3 238.2 all-reduce.1
where the time goes:
time: 775 us; the launch traced here: 774 us
  waiting for transfers between devices  653 us (84%)
  other arithmetic  46.9 us (6%)
  local copies, waits for them, and re-layouts  35.5 us (5%)
  matrix products  23.9 us (3%)
  between operations  14.5 us (2%)
    psum x1, waiting for transfers between devices, body(): grad_weight = lax.psum(local_grad, ('row', 'col'))  240 us
    all_gather x1, waiting for transfers between devices, body(): gathered = lax.all_gather(scaled_in, 'row', axis=0, tiled=True)  160 us
    reduce_scatter x1, waiting for transfers between devices, body(): lax.psum_scatter(partial_cols, 'row', scatter_dimension=0, tiled=True)  156 us
    reduce_scatter x1, waiting for transfers between devices, body(): lax.psum_scatter(partial_rows, 'col', scatter_dimension=0, tiled=True)  62.7 us
    scatter-add x2, other arithmetic, place_tiles(): jnp.zeros((out_tiles, tile, width), jnp.float32).at[places]  43.6 us
    all_gather x1, waiting for transfers between devices, body(): grad_rows = lax.all_gather(scaled_grad, 'col', axis=0, tiled=True)  33.5 us
    mul x2, local copies, waits for them, and re-layouts, tile_products(): return prods * weights[:, None, None]  18 us
  transfers between devices with their start and end apart: 5, of which 5 were waited for; matrix products, arithmetic and copies ran while one was open for 0% of the time, Pallas kernels for 0%

commit v1 on v0

v1 whole, which is shorter than its diff:
```python
import jax
import jax.numpy as jnp
from jax import lax
from jax.experimental import pallas as pl
from jax.experimental.pallas import tpu as pltpu
from jax.sharding import PartitionSpec as P

MESH = pl.DeviceIdType.MESH
T = 128
F32 = jnp.float32
BF16 = jnp.bfloat16
ROW_MSGS = 31


def ring(place, step):
    return lax.rem(place + step, 4)


def send(src, dst, ssem, rsem, device):
    pltpu.make_async_remote_copy(
        src_ref=src, dst_ref=dst, send_sem=ssem, recv_sem=rsem, device_id=device, device_id_type=MESH
    ).start()


def sent(src, ssem, rsem, device):
    pltpu.make_async_remote_copy(
        src_ref=src, dst_ref=src, send_sem=ssem, recv_sem=rsem, device_id=device, device_id_type=MESH
    ).wait_send()


def arrived(dst, ssem, rsem, device):
    pltpu.make_async_remote_copy(
        src_ref=dst, dst_ref=dst, send_sem=ssem, recv_sem=rsem, device_id=device, device_id_type=MESH
    ).wait_recv()


def kernel(
    feat, weight, cot, values, coords, count, rdeg, cdeg, out_ref, gin_ref, gw_ref,
    X, V, G, D, R, Q, F, acc, vtab, stab, cscale, rscale,
    b1, b2, b3, c1, e1, x1, x2, x3, xc, e2, bz,
    h1, he, u1, u2, u3, uc,
    w0, a1, a2, a3, a4, s1, s2, full,
    load_sem, tab_sem, row_s, row_r, sum_s, sum_r, col_s, col_r, fsum_s, fsum_r, ar_s, ar_r,
):
    r, c = lax.axis_index("row"), lax.axis_index("col")
    zl, y, x = r // 16, lax.rem(r // 4, 4), lax.rem(r, 4)
    zh, core = c // 2, lax.rem(c, 2)
    z = zh * 2 + zl

    def place(q):
        return x + q * (y - x), y + q * (x - y)

    def row_of(q, zu, p1, p2):
        return zu * 16 + p1 * (1 + 3 * q) + p2 * (4 - 3 * q)

    def unit(ref, q, zu, p1, p2):
        return ref.at[pl.ds(4 * row_of(q, zu, p1, p2) + 2 * q, 2)]

    def on_first(q, step):
        p1, p2 = place(q)
        return (row_of(q, zl, ring(p1, step), p2), c)

    def on_second(q, step):
        p1, p2 = place(q)
        return (row_of(q, zl, p1, ring(p2, step)), c)

    def on_zh(step):
        return (r, ring(zh, step) * 2 + core)

    def on_z(step):
        other = lax.rem(z + step, 8)
        return (lax.rem(other, 2) * 16 + y * 4 + x, (other // 2) * 2 + core)

    partner = ((1 - zl) * 16 + y * 4 + x, c)
    sibling = (r, zh * 2 + 1 - core)
    near, far = zl, 1 - zl
    halves = (0, 1)

    def loop(n, fn):
        def step(i, carry):
            fn(i)
            return carry

        lax.fori_loop(0, n, step, 0)

    def each_half(fn):
        loop(2, fn)

    def each_unit(fn, first=near):
        loop(4, lambda i: fn(lax.rem(i, 2), first + (i // 2) * (1 - 2 * first)))

    load = pltpu.make_async_copy(values, V, load_sem)
    load.start()

    barrier = pltpu.get_barrier_semaphore()
    friends = [sibling]
    friends += [on_first(0, d) for d in (1, 2, 3)]
    friends += [on_first(1, d) for d in (1, 2, 3)]
    friends += [on_z(d) for d in range(1, 8)]
    for friend in friends:
        pl.semaphore_signal(barrier, inc=1, device_id=friend, device_id_type=MESH)

    for k in range(4):
        for deg, scale in ((cdeg, cscale), (rdeg, rscale)):
            line = 1.0 / jnp.sqrt(deg[k : k + 1, :].astype(F32))
            scale[k] = jnp.transpose(jnp.broadcast_to(line, (T, T)))
    for k in range(4):
        rows = pl.ds(k * T, T)
        X[4 * r + k] = (feat[rows, :].astype(F32) * cscale[k]).astype(BF16)
        grad = lax.dot_general(cot[rows, :], weight[...], (((1,), (1,)), ((), ())), preferred_element_type=F32)
        G[4 * c + k] = (rscale[k] * grad).astype(BF16)

    pl.semaphore_wait(barrier, len(friends))

    def row_index1(q, zu, k):
        return q * ROW_MSGS + zu * 3 + k

    def row_index2(q, zu, o, k):
        return q * ROW_MSGS + 6 + (zu * 4 + o) * 3 + k

    def row_indexz(q):
        return q * ROW_MSGS + 30

    def route(zu, k):
        if k == 0:
            return 0, 1
        if k == 1:
            return 0, 3
        return 3 - 2 * zu, 1 + 2 * zu

    def gather1(q, zu, k):
        p1, p2 = place(q)
        back, ahead = route(zu, k)
        piece = unit(X, q, zu, ring(p1, back), p2)
        i = row_index1(q, zu, k)
        send(piece, piece, row_s.at[i], row_r.at[i], on_first(q, ahead))

    def gathered1(q, zu, k):
        p1, p2 = place(q)
        piece = unit(X, q, zu, ring(p1, (3, 1, 2)[k]), p2)
        i = row_index1(q, zu, k)
        arrived(piece, row_s.at[i], row_r.at[i], on_first(q, 1))

    def gather2(q, zu, o, k):
        p1, p2 = place(q)
        back, ahead = route(zu, k)
        piece = unit(X, q, zu, ring(p1, o), ring(p2, back))
        i = row_index2(q, zu, o, k)
        send(piece, piece, row_s.at[i], row_r.at[i], on_second(q, ahead))

    def gathered2(q, zu, o, k):
        p1, p2 = place(q)
        piece = unit(X, q, zu, ring(p1, o), ring(p2, (3, 1, 2)[k]))
        i = row_index2(q, zu, o, k)
        arrived(piece, row_s.at[i], row_r.at[i], on_second(q, 1))

    def shard(ref, zh_of, core_of, first=0, tiles=4):
        return ref.at[pl.ds(4 * (zh_of * 2 + core_of) + first, tiles)]

    def col_piece(owner_step, i, core_of):
        if i in (2, 3, 7, 8):
            return shard(G, ring(zh, owner_step), core_of, 2 * ((i + 1) % 2) if i > 4 else 2 * (i - 2), 2)
        return shard(G, ring(zh, owner_step), core_of)

    def col_send(owner_step, i, device):
        piece = col_piece(owner_step, i, core)
        send(piece, piece, col_s.at[i], col_r.at[i], device)

    def col_arrived(i):
        piece = col_piece((3, 1, 2, 2, 0, 3, 1, 2, 2)[i], i, core if i < 4 else 1 - core)
        arrived(piece, col_s.at[i], col_r.at[i], on_zh(1) if i < 4 else sibling)

    @each_half
    def _(q):
        p1, p2 = place(q)
        piece = unit(X, q, near, p1, p2)
        i = row_indexz(q)
        send(piece, piece, row_s.at[i], row_r.at[i], partner)
        gather1(q, near, 0)
        gather1(q, near, 1)

    col_send(0, 0, on_zh(1))
    col_send(0, 1, on_zh(3))
    col_send(0, 4, sibling)

    @each_half
    def _(q):
        gather2(q, near, 0, 0)
        gather2(q, near, 0, 1)

    own = lax.broadcasted_iota(jnp.int32, (T, T), 0)
    lane = lax.broadcasted_iota(jnp.int32, (T, T), 1)
    live = own < count[0, 0]
    tile_row = jnp.broadcast_to(coords[:, 0:1], (T, T))
    tile_col = jnp.broadcast_to(coords[:, 1:2], (T, T))

    def pick(mask, what):
        return jnp.sum(jnp.where(mask, what, 0), axis=0, keepdims=True)

    for base, major, other in ((0, tile_col, tile_row), (8, tile_row, tile_col)):
        major = jnp.where(live, major, T)
        key = major * T + own
        rank = pick(key < jnp.transpose(key), jnp.ones_like(key))
        rank = jnp.transpose(jnp.broadcast_to(rank, (T, T)))
        here = rank == lane
        target = pick(here, major)
        before = pick(rank + 1 == lane, major + 1) - 1
        vtab[base : base + 1, :] = pick(here, own)
        vtab[base + 1 : base + 2, :] = pick(here, other)
        vtab[base + 2 : base + 3, :] = (target == before).astype(jnp.int32)
        vtab[base + 3 : base + 4, :] = jnp.maximum(pick(major <= lane, jnp.ones_like(key)) - 1, 0)
        vtab[base + 4 : base + 5, :] = jnp.minimum(pick(major == lane, jnp.ones_like(key)), 1)
    table = pltpu.make_async_copy(vtab, stab, tab_sem)
    table.start()

    def products(base, first, last, source, out, contract):
        def step(k, carry):
            tile = V[stab[base, k]]
            rows = source[stab[base + 1, k]]
            prod = lax.dot_general(tile, rows, (((contract,), (0,)), ((), ())), preferred_element_type=F32)
            total = prod + jnp.where(stab[base + 2, k] == 1, acc[...], 0.0)
            acc[...] = total
            out[k] = total.astype(BF16)
            return carry

        lax.fori_loop(first, last, step, 0, unroll=4)

    def spread(base, tiles, segments, out):
        def step(j, carry):
            out[j] = jnp.where(stab[base + 4, j] == 1, segments[stab[base + 3, j]], 0.0).astype(BF16)
            return carry

        lax.fori_loop(0, tiles, step, 0, unroll=4)

    @each_half
    def _(q):
        p1, p2 = place(q)
        i = row_indexz(q)
        arrived(unit(X, q, far, p1, p2), row_s.at[i], row_r.at[i], partner)
        gather1(q, far, 0)
        gather1(q, far, 1)
        gather2(q, far, 0, 0)
        gather2(q, far, 0, 1)

    col_arrived(0)
    col_send(3, 2, on_zh(1))
    col_send(3, 5, sibling)
    col_arrived(1)
    col_send(1, 3, on_zh(3))
    col_send(1, 6, sibling)

    @each_unit
    def _(q, zu):
        gathered1(q, zu, 0)
        gathered1(q, zu, 1)
        gather1(q, zu, 2)
        for o in (3, 1):
            gather2(q, zu, o, 0)
            gather2(q, zu, o, 1)

    col_arrived(2)
    col_send(2, 7, sibling)
    col_arrived(3)
    col_send(2, 8, sibling)

    @each_unit
    def _(q, zu):
        gathered2(q, zu, 0, 0)
        gathered2(q, zu, 0, 1)
        gather2(q, zu, 0, 2)

    @each_unit
    def _(q, zu):
        gathered1(q, zu, 2)
        gather2(q, zu, 2, 0)
        gather2(q, zu, 2, 1)

    for i in range(4, 9):
        col_arrived(i)
    load.wait()
    table.wait()
    acc[...] = jnp.zeros_like(acc)
    products(0, 0, 64, G, R, 0)

    @each_unit
    def _(q, zu):
        for o in (3, 1):
            gathered2(q, zu, o, 0)
            gathered2(q, zu, o, 1)
            gather2(q, zu, o, 2)

    products(0, 64, 128, G, R, 0)

    @each_unit
    def _(q, zu):
        gathered2(q, zu, 2, 0)
        gathered2(q, zu, 2, 1)
        gather2(q, zu, 2, 2)

    spread(0, 128, R, D)

    def sum_index(kind, q, zu, o):
        return ((kind * 2 + q) * 2 + zu) * 4 + o

    def sum_index2(kind, q, zu):
        return 48 + (kind * 2 + q) * 2 + zu

    def ahead_of(zu):
        return 1 + 2 * zu

    def behind_of(zu):
        return 3 - 2 * zu

    def sum_send(kind, q, zu, o):
        p1, p2 = place(q)
        step = behind_of(zu) if kind == 1 else ahead_of(zu)
        if kind == 2:
            src = c1.at[q, zu, o]
        else:
            src = unit(D, q, zu, ring(p1, o), ring(p2, 2 if kind == 0 else step))
        i = sum_index(kind, q, zu, o)
        send(src, (b1, b2, b3)[kind].at[q, zu, o], sum_s.at[i], sum_r.at[i], on_second(q, step))

    def sum_arrived(kind, q, zu, o):
        i = sum_index(kind, q, zu, o)
        arrived((b1, b2, b3)[kind].at[q, zu, o], sum_s.at[i], sum_r.at[i], on_second(q, 1))

    def sum_send2(kind, q, zu):
        step = behind_of(zu) if kind == 1 else ahead_of(zu)
        src = (e1.at[q, zu, 2], e1.at[q, zu, step], xc.at[q, zu])[kind]
        i = sum_index2(kind, q, zu)
        send(src, (x1, x2, x3)[kind].at[q, zu], sum_s.at[i], sum_r.at[i], on_first(q, step))

    def sum_arrived2(kind, q, zu):
        i = sum_index2(kind, q, zu)
        arrived((x1, x2, x3)[kind].at[q, zu], sum_s.at[i], sum_r.at[i], on_first(q, 1))

    def own_unit(q, zu, o, step):
        p1, p2 = place(q)
        return unit(D, q, zu, ring(p1, o), ring(p2, step))[...].astype(F32)

    order = (2, 1, 3, 0)
    for kind in (0, 1):
        for o in order:
            each_unit(lambda q, zu: sum_send(kind, q, zu, o), far)

    @each_unit
    def _(q, zu):
        for o in range(4):
            gathered2(q, zu, o, 2)

    acc[...] = jnp.zeros_like(acc)
    products(8, 0, 128, X, Q, 1)
    spread(8, 32, Q, F)

    def fsum_send(kind, h):
        step = (1 if h == 0 else 3) if kind != 1 else (3 if h == 0 else 1)
        src = (he.at[ring(zh, 2), pl.ds(2 * h, 2)], he.at[ring(zh, step), pl.ds(2 * h, 2)], uc.at[h])[kind]
        i = 4 + 2 * kind + h
        send(src, (u1, u2, u3)[kind].at[h], fsum_s.at[i], fsum_r.at[i], on_zh(step))

    def fsum_arrived(kind, h):
        i = 4 + 2 * kind + h
        arrived((u1, u2, u3)[kind].at[h], fsum_s.at[i], fsum_r.at[i], on_zh(1))

    for d in order:
        owner = ring(zh, d)
        send(shard(F, owner, 1 - core), h1.at[owner], fsum_s.at[d], fsum_r.at[d], sibling)

    for o in order:

        def relay(q, zu):
            sum_arrived(0, q, zu, o)
            c1[q, zu, o] = (b1[q, zu, o].astype(F32) + own_unit(q, zu, o, ahead_of(zu))).astype(BF16)
            sum_send(2, q, zu, o)

        each_unit(relay, far)

    for d in order:
        owner = ring(zh, d)
        arrived(h1.at[owner], fsum_s.at[d], fsum_r.at[d], sibling)
        he[owner] = (h1[owner].astype(F32) + shard(F, owner, core)[...].astype(F32)).astype(BF16)
        if d == 2:
            fsum_send(0, 0)
            fsum_send(0, 1)
    fsum_send(1, 0)
    fsum_send(1, 1)

    def total1(o):
        def add(q, zu):
            sum_arrived(1, q, zu, o)
            sum_arrived(2, q, zu, o)
            e1[q, zu, o] = (
                own_unit(q, zu, o, 0) + b2[q, zu, o].astype(F32) + b3[q, zu, o].astype(F32)
            ).astype(BF16)

        each_unit(add, far)

    total1(2)
    each_unit(lambda q, zu: sum_send2(0, q, zu), far)
    for h in halves:
        fsum_arrived(0, h)
        step = 1 if h == 0 else 3
        uc[h] = (u1[h].astype(F32) + he[ring(zh, step), pl.ds(2 * h, 2)].astype(F32)).astype(BF16)
        fsum_send(2, h)
    total1(1)
    total1(3)
    each_unit(lambda q, zu: sum_send2(1, q, zu), far)

    @each_unit
    def _(q, zu):
        sum_arrived2(0, q, zu)
        xc[q, zu] = (x1[q, zu].astype(F32) + e1[q, zu, ahead_of(zu)].astype(F32)).astype(BF16)
        sum_send2(2, q, zu)

    grad = jnp.zeros((T, T), F32)
    for h in halves:
        fsum_arrived(1, h)
        fsum_arrived(2, h)
        for k in (0, 1):
            n = 2 * h + k
            hidden = he[zh, n].astype(F32) + u2[h, k].astype(F32) + u3[h, k].astype(F32)
            hidden = (rscale[n] * hidden).astype(BF16)
            rows = pl.ds(n * T, T)
            out_ref[rows, :] = jnp.dot(hidden, weight[...], preferred_element_type=F32).astype(BF16)
            grad += lax.dot_general(hidden, cot[rows, :], (((0,), (0,)), ((), ())), preferred_element_type=F32)
    w0[...] = grad

    def ar_send(i, src, dst, device):
        send(src, dst, ar_s.at[i], ar_r.at[i], device)

    def ar_arrived(i, dst, device):
        arrived(dst, ar_s.at[i], ar_r.at[i], device)

    def on_x(d):
        return on_first(0, d)

    def on_y(d):
        return on_first(1, d)

    ar_send(0, w0.at[pl.ds((1 - core) * 64, 64)], a1, sibling)
    total1(0)
    ar_arrived(0, a1, sibling)
    s1[...] = a1[...] + w0[pl.ds(core * 64, 64), :]
    for d in (1, 2, 3):
        ar_send(d, s1.at[pl.ds(ring(x, d) * 16, 16)], a2.at[d - 1], on_x(d))

    def total2(q, zu):
        sum_arrived2(1, q, zu)
        sum_arrived2(2, q, zu)
        return e1[q, zu, 0].astype(F32) + x2[q, zu].astype(F32) + x3[q, zu].astype(F32)

    @each_half
    def _(q):
        e2[q] = total2(q, far).astype(BF16)
        send(e2.at[q], bz.at[q], sum_s.at[60 + q], sum_r.at[60 + q], partner)

    for d in (1, 2, 3):
        ar_arrived(d, a2.at[d - 1], on_x(d))
    a3[y] = s1[pl.ds(x * 16, 16), :] + a2[0] + a2[1] + a2[2]
    for d in (1, 2, 3):
        ar_send(3 + d, a3.at[y], a3.at[y], on_y(d))
    for d in (1, 2, 3):
        ar_arrived(3 + d, a3.at[ring(y, 4 - d)], on_y(d))
    a4[z] = a3[0] + a3[1] + a3[2] + a3[3]
    for d in range(1, 8):
        ar_send(6 + d, a4.at[z], a4.at[z], on_z(d))

    @each_half
    def _(q):
        mine = total2(q, near)
        arrived(bz.at[q], sum_s.at[60 + q], sum_r.at[60 + q], partner)
        mine = mine + bz[q].astype(F32)
        for k in (0, 1):
            n = 2 * q + k
            gin_ref[pl.ds(n * T, T), :] = (cscale[n] * mine[k]).astype(BF16)

    for d in range(1, 8):
        ar_arrived(6 + d, a4.at[lax.rem(z + 8 - d, 8)], on_z(d))
    s2[...] = a4[0] + a4[1] + a4[2] + a4[3] + a4[4] + a4[5] + a4[6] + a4[7]
    mine = pl.ds(core * 64 + x * 16, 16)
    for d in (1, 2, 3):
        ar_send(13 + d, s2, full.at[mine], on_x(d))
    full[mine, :] = s2[...]
    for d in (1, 2, 3):
        ar_arrived(13 + d, full.at[pl.ds(core * 64 + ring(x, 4 - d) * 16, 16)], on_x(d))
    half = full.at[pl.ds(core * 64, 64)]
    ar_send(17, half, half, sibling)
    ar_arrived(17, full.at[pl.ds((1 - core) * 64, 64)], sibling)
    gw_ref[...] = full[...]

    loop(62, lambda i: sent(X.at[pl.ds(0, 2)], row_s.at[i], row_r.at[i], sibling))
    loop(62, lambda i: sent(D.at[pl.ds(0, 2)], sum_s.at[i], sum_r.at[i], sibling))
    for i in range(9):
        sent(G.at[pl.ds(0, 2 if i in (2, 3, 7, 8) else 4)], col_s.at[i], col_r.at[i], sibling)
    for i in range(10):
        sent(F.at[pl.ds(0, 4 if i < 4 else 2)], fsum_s.at[i], fsum_r.at[i], sibling)
    for i in range(18):
        sent(full.at[pl.ds(0, 64 if i in (0, 17) else 16)], ar_s.at[i], ar_r.at[i], sibling)


def body(features, weight, cotangent, tile_values, tile_coords, tile_count, row_degree, col_degree):
    vmem = pl.BlockSpec(memory_space=pltpu.VMEM)
    units = lambda *lead: pltpu.VMEM((*lead, 2, T, T), BF16)
    sems = lambda n: pltpu.SemaphoreType.DMA((n,))
    rows = lambda n: pltpu.VMEM((n, T), F32)
    return pl.pallas_call(
        kernel,
        out_shape=(
            jax.ShapeDtypeStruct((512, T), BF16),
            jax.ShapeDtypeStruct((512, T), BF16),
            jax.ShapeDtypeStruct((T, T), F32),
        ),
        in_specs=[
            vmem, vmem, vmem, pl.BlockSpec(memory_space=pl.ANY), vmem,
            pl.BlockSpec(memory_space=pltpu.SMEM), vmem, vmem,
        ],
        out_specs=(vmem, vmem, vmem),
        scratch_shapes=[
            pltpu.VMEM((128, T, T), BF16),
            pltpu.VMEM((128, T, T), BF16),
            pltpu.VMEM((32, T, T), BF16),
            pltpu.VMEM((128, T, T), BF16),
            pltpu.VMEM((128, T, T), BF16),
            pltpu.VMEM((128, T, T), BF16),
            pltpu.VMEM((32, T, T), BF16),
            rows(T),
            pltpu.VMEM((16, T), jnp.int32),
            pltpu.SMEM((16, T), jnp.int32),
            pltpu.VMEM((4, T, T), F32),
            pltpu.VMEM((4, T, T), F32),
            units(2, 2, 4), units(2, 2, 4), units(2, 2, 4), units(2, 2, 4), units(2, 2, 4),
            units(2, 2), units(2, 2), units(2, 2), units(2, 2), units(2), units(2),
            pltpu.VMEM((4, 4, T, T), BF16),
            pltpu.VMEM((4, 4, T, T), BF16),
            units(2), units(2), units(2), units(2),
            rows(T),
            rows(64),
            pltpu.VMEM((3, 16, T), F32),
            pltpu.VMEM((4, 16, T), F32),
            pltpu.VMEM((8, 16, T), F32),
            rows(64),
            rows(16),
            rows(T),
            pltpu.SemaphoreType.DMA, pltpu.SemaphoreType.DMA,
            sems(62), sems(62), sems(62), sems(62), sems(9), sems(9), sems(10), sems(10), sems(18), sems(18),
        ],
        compiler_params=pltpu.CompilerParams(
            collective_id=0, has_side_effects=True, vmem_limit_bytes=56 * 1024 * 1024
        ),
    )(
        features,
        weight,
        cotangent,
        tile_values[0, 0],
        tile_coords[0, 0],
        tile_count,
        row_degree.reshape(4, T),
        col_degree.reshape(4, T),
    )


def solution(mesh):
    in_specs = (
        P(("col", "row"), None),
        P(),
        P(("row", "col"), None),
        P("row", "col", None, None, None),
        P("row", "col", None, None),
        P("row", "col"),
        P(("row", "col")),
        P(("col", "row")),
    )
    out_specs = (P(("row", "col"), None), P(("col", "row"), None), P())
    return jax.shard_map(body, mesh=mesh, in_specs=in_specs, out_specs=out_specs, check_vma=False)
```

time: 775 us -> 92.8 us (0.12)
  waiting for transfers between devices: 653 us -> 0 us
  Pallas kernels: 0 us -> 85.2 us
  other arithmetic: 46.9 us -> 0 us
  local copies, waits for them, and re-layouts: 35.5 us -> 6.02 us
  matrix products: 23.9 us -> 0 us
  between operations: 14.5 us -> 1.29 us
    psum x1 -> x0, waiting for transfers between devices: 240 us -> none  [body(): grad_weight = lax.psum(local_grad, ('row', 'col'))]
    reduce_scatter x2 -> x0, waiting for transfers between devices: 219 us -> none  [the longest x1 156 us: body(): lax.psum_scatter(partial_cols, 'row', scatter_dimension=0, tiled=True)]
    all_gather x2 -> x0, waiting for transfers between devices: 193 us -> none  [the longest x1 160 us: body(): gathered = lax.all_gather(scaled_in, 'row', axis=0, tiled=True)]
    pallas_call x0 -> x1, Pallas kernels: none -> 85.2 us  [body(): pl.pallas_call(kernel, out_shape=(jax.ShapeDtypeStruct((512, T), BF16), j...]
    scatter-add x2 -> x0, other arithmetic: 43.6 us -> none  [place_tiles(): jnp.zeros((out_tiles, tile, width), jnp.float32).at[places]]
    dot_general x5 -> x0, matrix products: 23.9 us -> none  [the longest x1 9.81 us: tile_products(): jnp.einsum('tij,tjf->tif', values, picked, preferred_element_type=jnp.flo...]
    mul x2 -> x0, local copies, waits for them, and re-layouts: 18 us -> none  [tile_products(): return prods * weights[:, None, None]]
    gather x2 -> x0, local copies, waits for them, and re-layouts: 9.48 us -> none  [tile_products(): picked = in_tiles[coords[:, pick_dim]]]
  transfers between devices with their start and end apart: 5 -> 0, of which waited for: 5 -> 0; matrix products, arithmetic and copies ran while one was open for 0% -> 0% of each run, Pallas kernels for 0% -> 0%
where the time goes in v1:
time: 92.8 us; the launch traced here: 92.6 us
  Pallas kernels  85.2 us (92%)
  local copies, waits for them, and re-layouts  6.02 us (6%)
  between operations  1.29 us (1%)
    pallas_call x1, Pallas kernels, body(): pl.pallas_call(kernel, out_shape=(jax.ShapeDtypeStruct((512, T), BF16), j...  85.2 us
    unnamed x4, local copies, waits for them, and re-layouts  6.02 us

profile of v1, /device:TPU:1, one launch (start us, length us, event | category | flops | bytes accessed | tf_op | source)
XLA Modules:
  0.0 92.6 jit_solution(17442271162401093430)
XLA Ops:
  1.3 1.4 %copy.11 = s32[1,1,128,2]{3,2,1,0:T(8,128)} copy(s32[1,1,128,2]{2,3,1,0:T(2,128)} %param.12) | data formatting | bytes 2048 | tf_op args[4]
  2.7 85.2 %shard_map.103 = (bf16[512,128]{1,0:T(8,128)(2,1)}, bf16[512,128]{1,0:T(8,128)(2,1)}, f32[128,128]{1,0:T(8,128)}) custom-call(bf16[512,128]{1,0:T(8,128)(2,1)} %feat.1, bf16[128,128]{1,0:T(8,128)(2,1)} %weight.1, bf16[512,128]{1,0:T(8,128)(2,1)} %cot.1, bf16[128,128,128]{2,1,0:T(8,128)(2,1)} %bitcast.4, s32[128,2]{1,0:T(8,128)} %bitcast.5, ...), custom_call_target="tpu_custom_call" | custom-call | tf_op jit(solution)/shard_map/pallas_call | solution.py:507
  87.9 1.6 %copy.16 = bf16[512,128]{1,0:T(8,128)(2,1)} copy(bf16[512,128]{1,0:T(8,128)(2,1)} %get-tuple-element.6) | data formatting | bytes 262144
  89.5 1.6 %copy.17 = bf16[512,128]{1,0:T(8,128)(2,1)} copy(bf16[512,128]{1,0:T(8,128)(2,1)} %get-tuple-element.7) | data formatting | bytes 262144
  91.1 1.5 %copy.18 = f32[128,128]{1,0:T(8,128)} copy(f32[128,128]{1,0:T(8,128)} %get-tuple-element.8) | data formatting | bytes 131072

commit v2 on v0

v2 whole, which is shorter than its diff:
```python
import jax
import jax.numpy as jnp
from jax import lax
from jax.experimental import pallas as pl
from jax.experimental.pallas import tpu as pltpu
from jax.sharding import PartitionSpec as P

MESH = pl.DeviceIdType.MESH
T = 128
F32 = jnp.float32
BF16 = jnp.bfloat16


def ring(place, step):
    return lax.rem(place + step, 4)


def send(src, dst, ssem, rsem, device):
    pltpu.make_async_remote_copy(
        src_ref=src, dst_ref=dst, send_sem=ssem, recv_sem=rsem, device_id=device, device_id_type=MESH
    ).start()


def sent(src, ssem, rsem, device):
    pltpu.make_async_remote_copy(
        src_ref=src, dst_ref=src, send_sem=ssem, recv_sem=rsem, device_id=device, device_id_type=MESH
    ).wait_send()


def arrived(dst, ssem, rsem, device):
    pltpu.make_async_remote_copy(
        src_ref=dst, dst_ref=dst, send_sem=ssem, recv_sem=rsem, device_id=device, device_id_type=MESH
    ).wait_recv()


def kernel(
    feat, weight, cot, values, coords, count, rdeg, cdeg, out_ref, gin_ref, gw_ref,
    X, V, C, G, D, R, Q, F, acc, vtab, stab, cscale, rscale, fe, we, co, rd, cd, lo, gi,
    b1, b2, b3, c1, e1, x1, x2, x3, xc, e2, bz,
    h1, he, u1, u2, u3, uc,
    w0, a1, a2, a3, a4, s1, full, pad,
    load_sem, in_sem, out_sem, tab_sem, send_sem, row_r, sum_r, col_r, fsum_r, ar_r,
):
    r, c = lax.axis_index("row"), lax.axis_index("col")
    zl, y, x = r // 16, lax.rem(r // 4, 4), lax.rem(r, 4)
    zh, core = c // 2, lax.rem(c, 2)
    z = zh * 2 + zl

    px, py = [ring(x, d) for d in range(4)], [ring(y, d) for d in range(4)]
    on_x = [(zl * 16 + y * 4 + px[d], c) for d in range(4)]
    on_y = [(zl * 16 + py[d] * 4 + x, c) for d in range(4)]
    places = ((px, py), (py, px))
    devices = ((on_x, on_y), (on_y, on_x))

    def along(items, step):
        if isinstance(step, int):
            return items[step]
        return jnp.where(step == 1, items[1], items[3])

    def device(q, axis, step):
        there = devices[q][axis]
        if isinstance(step, int):
            return there[step]
        return (jnp.where(step == 1, there[1][0], there[3][0]), c)

    def unit(ref, q, zu, p1, p2):
        i, j = (p1, p2) if q == 0 else (p2, p1)
        return ref.at[pl.ds(64 * zu + 16 * j + 4 * i + 2 * q, 2)]

    def on_zh(step):
        return (r, ring(zh, step) * 2 + core)

    def on_z(step):
        other = lax.rem(z + step, 8)
        return (lax.rem(other, 2) * 16 + y * 4 + x, (other // 2) * 2 + core)

    partner = ((1 - zl) * 16 + y * 4 + x, c)
    sibling = (r, zh * 2 + 1 - core)
    near, far = zl, 1 - zl
    halves = (0, 1)

    ins = [
        pltpu.make_async_copy(src, dst, in_sem.at[i])
        for i, (src, dst) in enumerate(
            ((cdeg, cd), (feat, fe), (rdeg, rd), (cot, C.at[c, pl.ds(0, 512)]), (weight, we), (coords, co))
        )
    ]
    for copy in ins:
        copy.start()
    load = pltpu.make_async_copy(values, V, load_sem)
    load.start()

    barrier = pltpu.get_barrier_semaphore()
    friends = [sibling]
    friends += [on_x[d] for d in (1, 2, 3)]
    friends += [on_y[d] for d in (1, 2, 3)]
    friends += [on_z(d) for d in range(1, 8)]
    for friend in friends:
        pl.semaphore_signal(barrier, inc=1, device_id=friend, device_id_type=MESH)

    def column(line):
        return jnp.transpose(jnp.broadcast_to(1.0 / jnp.sqrt(line.astype(F32)), (T, T)))

    for copy in ins:
        copy.wait()
    for k in range(4):
        cscale[k] = column(cd[k : k + 1, :])
        X[4 * r + k] = (fe[pl.ds(k * T, T), :].astype(F32) * cscale[k]).astype(BF16)
    line = lax.broadcasted_iota(jnp.int32, (16, T), 0)
    tail = jnp.ones((16, T), F32)
    for k in range(4):
        tail = jnp.where(line == k, jnp.broadcast_to(rd[k : k + 1, :].astype(F32), (16, T)), tail)
    C[c, pl.ds(512, 16), :] = tail.astype(BF16)

    pl.semaphore_wait(barrier, len(friends))

    def route(zu, k):
        if k == 0:
            return 0, 1
        if k == 1:
            return 0, 3
        return 3 - 2 * zu, 1 + 2 * zu

    def gather1(q, zu, k):
        first, second = places[q]
        back, ahead = route(zu, k)
        piece = unit(X, q, zu, along(first, back), second[0])
        send(piece, piece, send_sem.at[0], row_r.at[6 * zu + k // 2], device(q, 0, ahead))

    def gather2(q, zu, o, k):
        first, second = places[q]
        back, ahead = route(zu, k)
        piece = unit(X, q, zu, first[o], along(second, back))
        i = 13 if k == 2 else 6 * zu + 2 + o
        send(piece, piece, send_sem.at[0], row_r.at[i], device(q, 1, ahead))

    def gathered(i, tiles):
        arrived(X.at[pl.ds(0, tiles)], send_sem.at[0], row_r.at[i], sibling)

    def shard(ref, zh_of, core_of):
        return ref.at[pl.ds(4 * (zh_of * 2 + core_of), 4)]

    def col_piece(owner_step, i, core_of):
        whose = ring(zh, owner_step) * 2 + core_of
        if i in (2, 7):
            return C.at[whose, pl.ds(0, 256)]
        if i in (3, 8):
            return C.at[whose, pl.ds(256, 272)]
        return C.at[whose]

    def col_send(owner_step, i, device):
        piece = col_piece(owner_step, i, core)
        send(piece, piece, send_sem.at[1], col_r.at[(0, 0, 1, 1, 2, 3, 3, 4, 4)[i]], device)

    def col_arrived(i):
        n = (2, 1, 1, 2, 1)[i]
        arrived(C.at[pl.ds(0, n)], send_sem.at[1], col_r.at[i], sibling)

    def scaled_grad(owner):
        lines = C[owner, pl.ds(512, 16), :].astype(F32)
        for k in range(4):
            n = 4 * owner + k
            scale = column(lines[k : k + 1, :])
            rscale[n] = scale
            grad = lax.dot_general(
                C[owner, pl.ds(k * T, T), :], we[...], (((1,), (1,)), ((), ())), preferred_element_type=F32
            )
            G[n] = (scale * grad).astype(BF16)

    for q in halves:
        piece = unit(X, q, near, places[q][0][0], places[q][1][0])
        send(piece, piece, send_sem.at[0], row_r.at[12], partner)
    for q in halves:
        gather1(q, near, 0)
        gather1(q, near, 1)
    for q in halves:
        gather2(q, near, 0, 0)
        gather2(q, near, 0, 1)
    col_send(0, 0, on_zh(1))
    col_send(0, 1, on_zh(3))
    col_send(0, 4, sibling)

    own = lax.broadcasted_iota(jnp.int32, (T, T), 0)
    lane = lax.broadcasted_iota(jnp.int32, (T, T), 1)
    live = own < count[0, 0]
    by_row = jnp.transpose(jnp.broadcast_to(co[0:1, :], (T, T)))
    by_col = jnp.transpose(jnp.broadcast_to(co[1:2, :], (T, T)))
    def pick(mask, what):
        return jnp.sum(jnp.where(mask, what, 0), axis=0, keepdims=True)

    for base, major, other in ((0, by_col, by_row), (8, by_row, by_col)):
        major = jnp.where(live, major, T)
        key = major * T + own
        rank = pick(key < jnp.transpose(key), jnp.ones_like(key))
        rank = jnp.transpose(jnp.broadcast_to(rank, (T, T)))
        here = rank == lane
        target = pick(here, major)
        before = pick(rank + 1 == lane, major + 1) - 1
        vtab[base : base + 1, :] = pick(here, own)
        vtab[base + 1 : base + 2, :] = pick(here, other)
        vtab[base + 2 : base + 3, :] = (target == before).astype(jnp.int32)
        vtab[base + 3 : base + 4, :] = jnp.maximum(pick(major <= lane, jnp.ones_like(key)) - 1, 0)
        vtab[base + 4 : base + 5, :] = jnp.minimum(pick(major == lane, jnp.ones_like(key)), 1)
    table = pltpu.make_async_copy(vtab, stab, tab_sem)
    table.start()

    def products(base, first, last, source, out, contract):
        def step(k, carry):
            tile = V[stab[base, k]]
            rows = source[stab[base + 1, k]]
            prod = lax.dot_general(tile, rows, (((contract,), (0,)), ((), ())), preferred_element_type=F32)
            total = prod + jnp.where(stab[base + 2, k] == 1, acc[...], 0.0)
            acc[...] = total
            out[k] = total.astype(out.dtype)
            return carry

        lax.fori_loop(first, last, step, 0, unroll=4)

    def segment(base, segments, j):
        return jnp.where(stab[base + 4, j] == 1, segments[stab[base + 3, j]], 0.0)

    def spread(first, last):
        def step(j, carry):
            D[j] = segment(0, R, j).astype(BF16)
            return carry

        lax.fori_loop(first, last, step, 0, unroll=4)

    def turn1(zu):
        gathered(6 * zu, 8)
        for q in halves:
            gather1(q, zu, 2)
        for o in (3, 1):
            for q in halves:
                gather2(q, zu, o, 0)
                gather2(q, zu, o, 1)

    def turn2(zu):
        gathered(6 * zu + 1, 4)
        for q in halves:
            gather2(q, zu, 2, 0)
            gather2(q, zu, 2, 1)

    def turn3(zu, o):
        gathered(6 * zu + 2 + o, 8)
        for q in halves:
            gather2(q, zu, o, 2)

    turn1(near)
    gathered(12, 4)
    for q in halves:
        gather1(q, far, 0)
        gather1(q, far, 1)
    for q in halves:
        gather2(q, far, 0, 0)
        gather2(q, far, 0, 1)
    turn2(near)
    turn1(far)
    turn3(near, 0)
    scaled_grad(c)
    col_arrived(2)
    scaled_grad(zh * 2 + 1 - core)
    turn2(far)
    turn3(near, 3)
    turn3(near, 1)
    col_arrived(0)
    col_send(3, 2, on_zh(1))
    col_send(1, 3, on_zh(3))
    col_send(3, 5, sibling)
    col_send(1, 6, sibling)
    turn3(far, 0)
    scaled_grad(ring(zh, 3) * 2 + core)
    scaled_grad(ring(zh, 1) * 2 + core)
    turn3(near, 2)
    col_arrived(3)
    scaled_grad(ring(zh, 3) * 2 + 1 - core)
    scaled_grad(ring(zh, 1) * 2 + 1 - core)
    turn3(far, 3)
    turn3(far, 1)
    col_arrived(1)
    col_send(2, 7, sibling)
    col_send(2, 8, sibling)
    scaled_grad(ring(zh, 2) * 2 + core)
    turn3(far, 2)
    col_arrived(4)
    scaled_grad(ring(zh, 2) * 2 + 1 - core)
    load.wait()
    table.wait()
    acc[...] = jnp.zeros_like(acc)
    products(0, 0, 128, G, R, 0)
    spread(0, 128)

    def ahead_of(zu):
        return 1 + 2 * zu

    def behind_of(zu):
        return 3 - 2 * zu

    def sum_send(kind, q, zu, o):
        first, second = places[q]
        step = behind_of(zu) if kind == 1 else ahead_of(zu)
        if kind == 2:
            src = c1.at[q, zu, o]
        else:
            src = unit(D, q, zu, first[o], second[2] if kind == 0 else along(second, step))
        i = o if kind == 0 else 4 + o
        send(src, (b1, b2, b3)[kind].at[q, zu, o], send_sem.at[2], sum_r.at[i], device(q, 1, step))

    def sum_arrived(i, tiles):
        arrived(D.at[pl.ds(0, tiles)], send_sem.at[2], sum_r.at[i], sibling)

    def sum_send2(kind, q, zu):
        step = behind_of(zu) if kind == 1 else ahead_of(zu)
        src = (e1.at[q, zu, 2], e1.at[q, zu, step], xc.at[q, zu])[kind]
        i = 8 if kind == 0 else 9 + zu
        send(src, (x1, x2, x3)[kind].at[q, zu], send_sem.at[2], sum_r.at[i], device(q, 0, step))

    def own_unit(q, zu, o, step):
        first, second = places[q]
        return unit(D, q, zu, first[o], along(second, step))[...].astype(F32)

    order = (2, 1, 3, 0)
    both = [(q, zu) for zu in (far, near) for q in halves]
    for kind in (0, 1):
        for o in order:
            for q, zu in both:
                sum_send(kind, q, zu, o)

    gathered(13, 32)

    def relay(o):
        sum_arrived(o, 8)
        for q, zu in both:
            c1[q, zu, o] = (b1[q, zu, o].astype(F32) + own_unit(q, zu, o, ahead_of(zu))).astype(BF16)
            sum_send(2, q, zu, o)

    def total1(o):
        sum_arrived(4 + o, 16)
        for q, zu in both:
            e1[q, zu, o] = (
                own_unit(q, zu, o, 0) + b2[q, zu, o].astype(F32) + b3[q, zu, o].astype(F32)
            ).astype(BF16)

    acc[...] = jnp.zeros_like(acc)
    products(8, 0, 64, X, Q, 1)
    relay(2)
    products(8, 64, 96, X, Q, 1)
    relay(1)
    products(8, 96, 128, X, Q, 1)

    def scaled(i, carry):
        F[i] = (rscale[i] * segment(8, Q, i)).astype(BF16)
        return carry

    lax.fori_loop(0, 32, scaled, 0, unroll=4)

    def fsum_send(kind, h):
        step = (1 if h == 0 else 3) if kind != 1 else (3 if h == 0 else 1)
        src = (he.at[ring(zh, 2), pl.ds(2 * h, 2)], he.at[ring(zh, step), pl.ds(2 * h, 2)], uc.at[h])[kind]
        send(src, (u1, u2, u3)[kind].at[h], send_sem.at[3], fsum_r.at[2 if kind == 0 else 3], on_zh(step))

    def fsum_arrived(i, tiles):
        arrived(F.at[pl.ds(0, tiles)], send_sem.at[3], fsum_r.at[i], sibling)

    for d in order:
        owner = ring(zh, d)
        send(shard(F, owner, 1 - core), h1.at[owner], send_sem.at[3], fsum_r.at[0 if d == 2 else 1], sibling)

    relay(3)
    w0[...] = jnp.zeros_like(w0)
    for owner in range(8):

        def share(k, carry):
            w0[...] += lax.dot_general(
                F[4 * owner + k],
                C[owner, pl.ds(pl.multiple_of(k * T, T), T), :],
                (((0,), (0,)), ((), ())),
                preferred_element_type=F32,
            )
            return carry

        lax.fori_loop(0, 4, share, 0, unroll=True)

    def ar_send(i, src, dst, device):
        send(src, dst, send_sem.at[4 if i in (0, 5) else 5], ar_r.at[i], device)

    def ar_arrived(i, dst):
        arrived(dst, send_sem.at[4], ar_r.at[i], sibling)

    def on_z_place(d):
        return lax.rem(z + d, 8)

    ar_send(0, w0.at[pl.ds((1 - core) * 64, 64)], a1, sibling)
    relay(0)
    fsum_arrived(0, 4)
    fsum_arrived(1, 12)
    for d in order:
        owner = ring(zh, d)
        he[owner] = (h1[owner].astype(F32) + shard(F, owner, core)[...].astype(F32)).astype(BF16)
        if d == 2:
            fsum_send(0, 0)
            fsum_send(0, 1)
    fsum_send(1, 0)
    fsum_send(1, 1)
    ar_arrived(0, a1)
    s1[...] = a1[...] + w0[pl.ds(core * 64, 64), :]
    for d in range(1, 8):
        ar_send(1, s1.at[pl.ds(on_z_place(d) * 8, 8)], a2.at[d - 1], on_z(d))
    fsum_arrived(2, 4)
    for h in halves:
        step = 1 if h == 0 else 3
        uc[h] = (u1[h].astype(F32) + he[ring(zh, step), pl.ds(2 * h, 2)].astype(F32)).astype(BF16)
        fsum_send(2, h)
    ar_arrived(1, a2)
    a3[y] = s1[pl.ds(z * 8, 8), :] + ((a2[0] + a2[1]) + (a2[2] + a2[3])) + ((a2[4] + a2[5]) + a2[6])
    for d in (1, 2, 3):
        ar_send(2, a3.at[y], a3.at[y], on_y[d])
    total1(2)
    for q, zu in both:
        sum_send2(0, q, zu)
    total1(1)
    total1(3)
    for q, zu in both:
        sum_send2(1, q, zu)
    ar_arrived(2, a2.at[pl.ds(0, 3)])
    a4[x] = (a3[0] + a3[1]) + (a3[2] + a3[3])
    for d in (1, 2, 3):
        ar_send(3, a4.at[x], a4.at[x], on_x[d])
    sum_arrived(8, 8)
    for q, zu in both:
        xc[q, zu] = (x1[q, zu].astype(F32) + e1[q, zu, ahead_of(zu)].astype(F32)).astype(BF16)
        sum_send2(2, q, zu)
    total1(0)

    fsum_arrived(3, 8)
    for n in range(4):
        h, k = n // 2, n % 2
        hidden = he[zh, n].astype(F32) + u2[h, k].astype(F32) + u3[h, k].astype(F32)
        rows = pl.ds(n * T, T)
        lo[rows, :] = jnp.dot(hidden.astype(BF16), we[...], preferred_element_type=F32).astype(BF16)
    outs = [pltpu.make_async_copy(lo, out_ref, out_sem.at[0])]
    outs[0].start()
    ar_arrived(3, a2.at[pl.ds(0, 3)])
    mine = pl.ds(core * 64 + z * 8, 8)
    full[mine, :] = (a4[0] + a4[1]) + (a4[2] + a4[3])
    for d in range(1, 8):
        ar_send(4, full.at[mine], full.at[mine], on_z(d))

    def total2(q, zu):
        return e1[q, zu, 0].astype(F32) + x2[q, zu].astype(F32) + x3[q, zu].astype(F32)

    sum_arrived(9 + far, 8)
    for q in halves:
        e2[q] = total2(q, far).astype(BF16)
        send(e2.at[q], bz.at[q], send_sem.at[2], sum_r.at[11], partner)
    ar_arrived(4, a2)
    half = full.at[pl.ds(core * 64, 64)]
    ar_send(5, half, half, sibling)
    ar_arrived(5, a1)
    outs.append(pltpu.make_async_copy(full, gw_ref, out_sem.at[1]))
    outs[1].start()
    sum_arrived(9 + near, 8)
    sum_arrived(11, 4)
    for q in halves:
        mine = total2(q, near) + bz[q].astype(F32)
        for k in (0, 1):
            n = 2 * q + k
            gi[pl.ds(n * T, T), :] = (cscale[n] * mine[k]).astype(BF16)
    outs.append(pltpu.make_async_copy(gi, gin_ref, out_sem.at[2]))
    outs[2].start()

    sent(X.at[pl.ds(0, 124)], send_sem.at[0], row_r.at[0], sibling)
    sent(C.at[pl.ds(0, 7)], send_sem.at[1], col_r.at[0], sibling)
    sent(D.at[pl.ds(0, 124)], send_sem.at[2], sum_r.at[0], sibling)
    sent(F.at[pl.ds(0, 28)], send_sem.at[3], fsum_r.at[0], sibling)
    sent(w0, send_sem.at[4], ar_r.at[0], sibling)
    sent(pad, send_sem.at[5], ar_r.at[0], sibling)
    for copy in outs:
        copy.wait()


def leave(*refs):
    n = len(refs) // 2
    for src, dst in zip(refs[:n], refs[n:]):
        dst[...] = src[...]


def body(features, weight, cotangent, tile_values, tile_coords, tile_count, row_degree, col_degree):
    units = lambda *lead: pltpu.VMEM((*lead, 2, T, T), BF16)
    sems = lambda n: pltpu.SemaphoreType.DMA((n,))
    rows = lambda n: pltpu.VMEM((n, T), F32)
    vmem = pl.BlockSpec(memory_space=pltpu.VMEM)
    anywhere = pl.BlockSpec(memory_space=pl.ANY)
    outs = (
        jax.ShapeDtypeStruct((512, T), BF16),
        jax.ShapeDtypeStruct((512, T), BF16),
        jax.ShapeDtypeStruct((T, T), F32),
    )
    results = pl.pallas_call(
        kernel,
        out_shape=outs,
        in_specs=[anywhere] * 5 + [pl.BlockSpec(memory_space=pltpu.SMEM), anywhere, anywhere],
        out_specs=(anywhere,) * 3,
        scratch_shapes=[
            pltpu.VMEM((128, T, T), BF16),
            pltpu.VMEM((128, T, T), BF16),
            pltpu.VMEM((8, 528, T), BF16),
            pltpu.VMEM((32, T, T), BF16),
            pltpu.VMEM((128, T, T), BF16),
            pltpu.VMEM((128, T, T), BF16),
            pltpu.VMEM((128, T, T), F32),
            pltpu.VMEM((32, T, T), BF16),
            rows(T),
            pltpu.VMEM((16, T), jnp.int32),
            pltpu.SMEM((16, T), jnp.int32),
            pltpu.VMEM((4, T, T), F32),
            pltpu.VMEM((32, T, T), F32),
            pltpu.VMEM((512, T), BF16),
            pltpu.VMEM((T, T), BF16),
            pltpu.VMEM((2, T), jnp.int32),
            pltpu.VMEM((4, T), jnp.int32),
            pltpu.VMEM((4, T), jnp.int32),
            pltpu.VMEM((512, T), BF16),
            pltpu.VMEM((512, T), BF16),
            units(2, 2, 4), units(2, 2, 4), units(2, 2, 4), units(2, 2, 4), units(2, 2, 4),
            units(2, 2), units(2, 2), units(2, 2), units(2, 2), units(2), units(2),
            pltpu.VMEM((4, 4, T, T), BF16),
            pltpu.VMEM((4, 4, T, T), BF16),
            units(2), units(2), units(2), units(2),
            rows(T),
            rows(64),
            pltpu.VMEM((7, 8, T), F32),
            pltpu.VMEM((4, 8, T), F32),
            pltpu.VMEM((4, 8, T), F32),
            rows(64),
            rows(T),
            rows(160),
            pltpu.SemaphoreType.DMA, sems(6), sems(3), pltpu.SemaphoreType.DMA,
            sems(6), sems(14), sems(12), sems(5), sems(4), sems(6),
        ],
        compiler_params=pltpu.CompilerParams(
            collective_id=0, has_side_effects=True, vmem_limit_bytes=60 * 1024 * 1024
        ),
    )(
        features,
        weight,
        cotangent,
        tile_values[0, 0],
        tile_coords[0, 0].T,
        tile_count,
        row_degree.reshape(4, T),
        col_degree.reshape(4, T),
    )
    return pl.pallas_call(
        leave,
        out_shape=outs,
        in_specs=[vmem] * 3,
        out_specs=(vmem,) * 3,
    )(*results)


def solution(mesh):
    in_specs = (
        P(("col", "row"), None),
        P(),
        P(("row", "col"), None),
        P("row", "col", None, None, None),
        P("row", "col", None, None),
        P("row", "col"),
        P(("row", "col")),
        P(("col", "row")),
    )
    out_specs = (P(("row", "col"), None), P(("col", "row"), None), P())
    return jax.shard_map(body, mesh=mesh, in_specs=in_specs, out_specs=out_specs, check_vma=False)
```

time: 775 us -> 78.4 us (0.10)
  waiting for transfers between devices: 653 us -> 0 us
  Pallas kernels: 0 us -> 77 us
  other arithmetic: 46.9 us -> 0 us
  local copies, waits for them, and re-layouts: 35.5 us -> 0 us
  matrix products: 23.9 us -> 0 us
  between operations: 14.5 us -> 1.29 us
    psum x1 -> x0, waiting for transfers between devices: 240 us -> none  [body(): grad_weight = lax.psum(local_grad, ('row', 'col'))]
    reduce_scatter x2 -> x0, waiting for transfers between devices: 219 us -> none  [the longest x1 156 us: body(): lax.psum_scatter(partial_cols, 'row', scatter_dimension=0, tiled=True)]
    all_gather x2 -> x0, waiting for transfers between devices: 193 us -> none  [the longest x1 160 us: body(): gathered = lax.all_gather(scaled_in, 'row', axis=0, tiled=True)]
    pallas_call x0 -> x2, Pallas kernels: none -> 77 us  [the longest x1 75.3 us: body(): pl.pallas_call(kernel, out_shape=outs, in_specs=[anywhere] * 5 + [pl.Bloc...]
    scatter-add x2 -> x0, other arithmetic: 43.6 us -> none  [place_tiles(): jnp.zeros((out_tiles, tile, width), jnp.float32).at[places]]
    dot_general x5 -> x0, matrix products: 23.9 us -> none  [the longest x1 9.81 us: tile_products(): jnp.einsum('tij,tjf->tif', values, picked, preferred_element_type=jnp.flo...]
    mul x2 -> x0, local copies, waits for them, and re-layouts: 18 us -> none  [tile_products(): return prods * weights[:, None, None]]
    gather x2 -> x0, local copies, waits for them, and re-layouts: 9.48 us -> none  [tile_products(): picked = in_tiles[coords[:, pick_dim]]]
  transfers between devices with their start and end apart: 5 -> 0, of which waited for: 5 -> 0; matrix products, arithmetic and copies ran while one was open for 0% -> 0% of each run, Pallas kernels for 0% -> 0%
where the time goes in v2:
time: 78.4 us; the launch traced here: 78.3 us
  Pallas kernels  77 us (98%)
  between operations  1.29 us (2%)
    pallas_call x1, Pallas kernels, body(): pl.pallas_call(kernel, out_shape=outs, in_specs=[anywhere] * 5 + [pl.Bloc...  75.3 us
    pallas_call x1, Pallas kernels, body(): pl.pallas_call(leave, out_shape=outs, in_specs=[vmem] * 3, out_specs=(vme...  1.7 us

profile of v2, /device:TPU:1, one launch (start us, length us, event | category | flops | bytes accessed | tf_op | source)
XLA Modules:
  0.0 78.3 jit_solution(16256061210959386310)
XLA Ops:
  1.3 75.3 %shard_map.103 = (bf16[512,128]{1,0:T(8,128)(2,1)}, bf16[512,128]{1,0:T(8,128)(2,1)}, f32[128,128]{1,0:T(8,128)}) custom-call(bf16[512,128]{1,0:T(8,128)(2,1)} %feat.1, bf16[128,128]{1,0:T(8,128)(2,1)} %weight.1, bf16[512,128]{1,0:T(8,128)(2,1)} %cot.1, bf16[128,128,128]{2,1,0:T(8,128)(2,1)} %bitcast.6, s32[2,128]{1,0:T(2,128)} %bitcast.9, ...), custom_call_target="tpu_custom_call" | custom-call | tf_op jit(solution)/shard_map/pallas_call | solution.py:499
  76.6 1.7 %shard_map.104 = (bf16[512,128]{1,0:T(8,128)(2,1)}, bf16[512,128]{1,0:T(8,128)(2,1)}, f32[128,128]{1,0:T(8,128)}) custom-call(bf16[512,128]{1,0:T(8,128)(2,1)} %get-tuple-element.6.refs_0_, bf16[512,128]{1,0:T(8,128)(2,1)} %get-tuple-element.7.refs_1_, f32[128,128]{1,0:T(8,128)} %get-tuple-element.8.refs_2_), custom_call_target="tpu_custom_call" | custom-call | tf_op jit(solution)/shard_map/pallas_call | solution.py:554

commit v3 on v2

--- a/solution.py
+++ b/solution.py
@@ -35,7 +35,7 @@
 
 def kernel(
     feat, weight, cot, values, coords, count, rdeg, cdeg, out_ref, gin_ref, gw_ref,
-    X, V, C, G, D, R, Q, F, acc, vtab, stab, cscale, rscale, fe, we, co, rd, cd, lo, gi,
+    cn, X, V, C, G, D, R, Q, F, acc, vtab, stab, cscale, rscale, fe, we, co, rd, cd, lo, gi,
     b1, b2, b3, c1, e1, x1, x2, x3, xc, e2, bz,
     h1, he, u1, u2, u3, uc,
     w0, a1, a2, a3, a4, s1, full, pad,
@@ -82,7 +82,7 @@
     ins = [
         pltpu.make_async_copy(src, dst, in_sem.at[i])
         for i, (src, dst) in enumerate(
-            ((cdeg, cd), (feat, fe), (rdeg, rd), (cot, C.at[c, pl.ds(0, 512)]), (weight, we), (coords, co))
+            ((cdeg, cd), (feat, fe), (rdeg, rd), (cot, C.at[c, pl.ds(0, 512)]), (weight, we), (coords, co), (count, cn))
         )
     ]
     for copy in ins:
@@ -182,7 +182,7 @@
 
     own = lax.broadcasted_iota(jnp.int32, (T, T), 0)
     lane = lax.broadcasted_iota(jnp.int32, (T, T), 1)
-    live = own < count[0, 0]
+    live = own < jnp.broadcast_to(cn[...], (T, T))
     by_row = jnp.transpose(jnp.broadcast_to(co[0:1, :], (T, T)))
     by_col = jnp.transpose(jnp.broadcast_to(co[1:2, :], (T, T)))
     def pick(mask, what):
@@ -255,12 +255,11 @@
         gather2(q, far, 0, 0)
         gather2(q, far, 0, 1)
     turn2(near)
-    turn1(far)
     turn3(near, 0)
     scaled_grad(c)
     col_arrived(2)
     scaled_grad(zh * 2 + 1 - core)
-    turn2(far)
+    turn1(far)
     turn3(near, 3)
     turn3(near, 1)
     col_arrived(0)
@@ -272,22 +271,24 @@
     scaled_grad(ring(zh, 3) * 2 + core)
     scaled_grad(ring(zh, 1) * 2 + core)
     turn3(near, 2)
+    turn2(far)
     col_arrived(3)
     scaled_grad(ring(zh, 3) * 2 + 1 - core)
     scaled_grad(ring(zh, 1) * 2 + 1 - core)
-    turn3(far, 3)
-    turn3(far, 1)
     col_arrived(1)
     col_send(2, 7, sibling)
     col_send(2, 8, sibling)
     scaled_grad(ring(zh, 2) * 2 + core)
-    turn3(far, 2)
     col_arrived(4)
     scaled_grad(ring(zh, 2) * 2 + 1 - core)
     load.wait()
     table.wait()
     acc[...] = jnp.zeros_like(acc)
-    products(0, 0, 128, G, R, 0)
+    products(0, 0, 48, G, R, 0)
+    turn3(far, 3)
+    turn3(far, 1)
+    products(0, 48, 128, G, R, 0)
+    turn3(far, 2)
     spread(0, 128)
 
     def ahead_of(zu):
@@ -342,11 +343,12 @@
             ).astype(BF16)
 
     acc[...] = jnp.zeros_like(acc)
-    products(8, 0, 64, X, Q, 1)
+    products(8, 0, 48, X, Q, 1)
     relay(2)
-    products(8, 64, 96, X, Q, 1)
+    products(8, 48, 88, X, Q, 1)
     relay(1)
-    products(8, 96, 128, X, Q, 1)
+    products(8, 88, 128, X, Q, 1)
+    relay(3)
 
     def scaled(i, carry):
         F[i] = (rscale[i] * segment(8, Q, i)).astype(BF16)
@@ -366,7 +368,6 @@
         owner = ring(zh, d)
         send(shard(F, owner, 1 - core), h1.at[owner], send_sem.at[3], fsum_r.at[0 if d == 2 else 1], sibling)
 
-    relay(3)
     w0[...] = jnp.zeros_like(w0)
     for owner in range(8):
 
@@ -382,55 +383,71 @@
         lax.fori_loop(0, 4, share, 0, unroll=True)
 
     def ar_send(i, src, dst, device):
-        send(src, dst, send_sem.at[4 if i in (0, 5) else 5], ar_r.at[i], device)
+        send(src, dst, send_sem.at[4 if i == 0 else 5], ar_r.at[i], device)
 
     def ar_arrived(i, dst):
         arrived(dst, send_sem.at[4], ar_r.at[i], sibling)
 
-    def on_z_place(d):
-        return lax.rem(z + d, 8)
-
-    ar_send(0, w0.at[pl.ds((1 - core) * 64, 64)], a1, sibling)
-    relay(0)
+    def z_rows(step):
+        return pl.ds(lax.rem(z + step, 8) * 16, 16)
+
+    def relay2(q, zu):
+        xc[q, zu] = (x1[q, zu].astype(F32) + e1[q, zu, ahead_of(zu)].astype(F32)).astype(BF16)
+        sum_send2(2, q, zu)
+
+    def total2(q, zu):
+        return e1[q, zu, 0].astype(F32) + x2[q, zu].astype(F32) + x3[q, zu].astype(F32)
+
+    ar_send(0, w0, a1, sibling)
     fsum_arrived(0, 4)
     fsum_arrived(1, 12)
     for d in order:
         owner = ring(zh, d)
         he[owner] = (h1[owner].astype(F32) + shard(F, owner, core)[...].astype(F32)).astype(BF16)
-        if d == 2:
-            fsum_send(0, 0)
-            fsum_send(0, 1)
-    fsum_send(1, 0)
-    fsum_send(1, 1)
     ar_arrived(0, a1)
-    s1[...] = a1[...] + w0[pl.ds(core * 64, 64), :]
+    s1[...] = a1[...] + w0[...]
     for d in range(1, 8):
-        ar_send(1, s1.at[pl.ds(on_z_place(d) * 8, 8)], a2.at[d - 1], on_z(d))
+        ar_send(1, s1.at[z_rows(d)], a2.at[d - 1], on_z(d))
+    for kind in (0, 1):
+        for h in halves:
+            fsum_send(kind, h)
+    ar_arrived(1, a2)
+    a3[y] = s1[z_rows(0), :] + ((a2[0] + a2[1]) + (a2[2] + a2[3])) + ((a2[4] + a2[5]) + a2[6])
+    for d in (1, 2, 3):
+        ar_send(2, a3.at[y], a3.at[y], on_y[d])
+    total1(2)
+    for q, zu in both:
+        sum_send2(0, q, zu)
+    relay(0)
     fsum_arrived(2, 4)
     for h in halves:
         step = 1 if h == 0 else 3
         uc[h] = (u1[h].astype(F32) + he[ring(zh, step), pl.ds(2 * h, 2)].astype(F32)).astype(BF16)
         fsum_send(2, h)
-    ar_arrived(1, a2)
-    a3[y] = s1[pl.ds(z * 8, 8), :] + ((a2[0] + a2[1]) + (a2[2] + a2[3])) + ((a2[4] + a2[5]) + a2[6])
-    for d in (1, 2, 3):
-        ar_send(2, a3.at[y], a3.at[y], on_y[d])
-    total1(2)
-    for q, zu in both:
-        sum_send2(0, q, zu)
     total1(1)
     total1(3)
-    for q, zu in both:
-        sum_send2(1, q, zu)
+    for q in halves:
+        sum_send2(1, q, far)
     ar_arrived(2, a2.at[pl.ds(0, 3)])
     a4[x] = (a3[0] + a3[1]) + (a3[2] + a3[3])
     for d in (1, 2, 3):
         ar_send(3, a4.at[x], a4.at[x], on_x[d])
     sum_arrived(8, 8)
-    for q, zu in both:
-        xc[q, zu] = (x1[q, zu].astype(F32) + e1[q, zu, ahead_of(zu)].astype(F32)).astype(BF16)
-        sum_send2(2, q, zu)
+    for q in halves:
+        relay2(q, far)
+    for q in halves:
+        sum_send2(1, q, near)
+    for q in halves:
+        relay2(q, near)
     total1(0)
+    ar_arrived(3, a2.at[pl.ds(0, 3)])
+    full[z_rows(0), :] = (a4[0] + a4[1]) + (a4[2] + a4[3])
+    for d in range(1, 8):
+        ar_send(4, full.at[z_rows(0)], full.at[z_rows(0)], on_z(d))
+    sum_arrived(9 + far, 8)
+    for q in halves:
+        e2[q] = total2(q, far).astype(BF16)
+        send(e2.at[q], bz.at[q], send_sem.at[2], sum_r.at[11], partner)
 
     fsum_arrived(3, 8)
     for n in range(4):
@@ -440,23 +457,7 @@
         lo[rows, :] = jnp.dot(hidden.astype(BF16), we[...], preferred_element_type=F32).astype(BF16)
     outs = [pltpu.make_async_copy(lo, out_ref, out_sem.at[0])]
     outs[0].start()
-    ar_arrived(3, a2.at[pl.ds(0, 3)])
-    mine = pl.ds(core * 64 + z * 8, 8)
-    full[mine, :] = (a4[0] + a4[1]) + (a4[2] + a4[3])
-    for d in range(1, 8):
-        ar_send(4, full.at[mine], full.at[mine], on_z(d))
-
-    def total2(q, zu):
-        return e1[q, zu, 0].astype(F32) + x2[q, zu].astype(F32) + x3[q, zu].astype(F32)
-
-    sum_arrived(9 + far, 8)
-    for q in halves:
-        e2[q] = total2(q, far).astype(BF16)
-        send(e2.at[q], bz.at[q], send_sem.at[2], sum_r.at[11], partner)
     ar_arrived(4, a2)
-    half = full.at[pl.ds(core * 64, 64)]
-    ar_send(5, half, half, sibling)
-    ar_arrived(5, a1)
     outs.append(pltpu.make_async_copy(full, gw_ref, out_sem.at[1]))
     outs[1].start()
     sum_arrived(9 + near, 8)
@@ -499,9 +500,10 @@
     results = pl.pallas_call(
         kernel,
         out_shape=outs,
-        in_specs=[anywhere] * 5 + [pl.BlockSpec(memory_space=pltpu.SMEM), anywhere, anywhere],
+        in_specs=[anywhere] * 8,
         out_specs=(anywhere,) * 3,
         scratch_shapes=[
+            pltpu.VMEM((1, 1), jnp.int32),
             pltpu.VMEM((128, T, T), BF16),
             pltpu.VMEM((128, T, T), BF16),
             pltpu.VMEM((8, 528, T), BF16),
@@ -528,14 +530,14 @@
             pltpu.VMEM((4, 4, T, T), BF16),
             units(2), units(2), units(2), units(2),
             rows(T),
-            rows(64),
-            pltpu.VMEM((7, 8, T), F32),
-            pltpu.VMEM((4, 8, T), F32),
-            pltpu.VMEM((4, 8, T), F32),
-            rows(64),
             rows(T),
-            rows(160),
-            pltpu.SemaphoreType.DMA, sems(6), sems(3), pltpu.SemaphoreType.DMA,
+            pltpu.VMEM((7, 16, T), F32),
+            pltpu.VMEM((4, 16, T), F32),
+            pltpu.VMEM((4, 16, T), F32),
+            rows(T),
+            rows(T),
+            rows(320),
+            pltpu.SemaphoreType.DMA, sems(7), sems(3), pltpu.SemaphoreType.DMA,
             sems(6), sems(14), sems(12), sems(5), sems(4), sems(6),
         ],
         compiler_params=pltpu.CompilerParams(

time: 78.4 us -> 69.9 us (0.89)
  Pallas kernels: 77 us -> 68.6 us
    pallas_call x1, Pallas kernels: 75.3 us -> 66.9 us  [body(): pl.pallas_call(kernel, out_shape=outs, in_specs=[anywhere] * 8, out_specs...]
where the time goes in v3:
time: 69.9 us; the launch traced here: 69.8 us
  Pallas kernels  68.6 us (98%)
  between operations  1.29 us (2%)
    pallas_call x1, Pallas kernels, body(): pl.pallas_call(kernel, out_shape=outs, in_specs=[anywhere] * 8, out_specs...  66.9 us
    pallas_call x1, Pallas kernels, body(): pl.pallas_call(leave, out_shape=outs, in_specs=[vmem] * 3, out_specs=(vme...  1.7 us

profile of v3, /device:TPU:1, one launch (start us, length us, event | category | flops | bytes accessed | tf_op | source)
XLA Modules:
  0.0 69.8 jit_solution(70516487382046015)
XLA Ops:
  1.3 66.9 %shard_map.103 = (bf16[512,128]{1,0:T(8,128)(2,1)}, bf16[512,128]{1,0:T(8,128)(2,1)}, f32[128,128]{1,0:T(8,128)}) custom-call(bf16[512,128]{1,0:T(8,128)(2,1)} %feat.1, bf16[128,128]{1,0:T(8,128)(2,1)} %weight.1, bf16[512,128]{1,0:T(8,128)(2,1)} %cot.1, bf16[128,128,128]{2,1,0:T(8,128)(2,1)} %bitcast.6, s32[2,128]{1,0:T(2,128)} %bitcast.9, ...), custom_call_target="tpu_custom_call" | custom-call | tf_op jit(solution)/shard_map/pallas_call | solution.py:500
  68.1 1.7 %shard_map.104 = (bf16[512,128]{1,0:T(8,128)(2,1)}, bf16[512,128]{1,0:T(8,128)(2,1)}, f32[128,128]{1,0:T(8,128)}) custom-call(bf16[512,128]{1,0:T(8,128)(2,1)} %get-tuple-element.6.refs_0_, bf16[512,128]{1,0:T(8,128)(2,1)} %get-tuple-element.7.refs_1_, f32[128,128]{1,0:T(8,128)} %get-tuple-element.8.refs_2_), custom_call_target="tpu_custom_call" | custom-call | tf_op jit(solution)/shard_map/pallas_call | solution.py:556

commit v4 on v3

--- a/solution.py
+++ b/solution.py
@@ -165,7 +165,7 @@
             grad = lax.dot_general(
                 C[owner, pl.ds(k * T, T), :], we[...], (((1,), (1,)), ((), ())), preferred_element_type=F32
             )
-            G[n] = (scale * grad).astype(BF16)
+            G[n] = jnp.transpose((scale * grad).astype(BF16))
 
     for q in halves:
         piece = unit(X, q, near, places[q][0][0], places[q][1][0])
@@ -205,16 +205,20 @@
     table.start()
 
     def products(base, first, last, source, out, contract):
-        def step(k, carry):
-            tile = V[stab[base, k]]
-            rows = source[stab[base + 1, k]]
-            prod = lax.dot_general(tile, rows, (((contract,), (0,)), ((), ())), preferred_element_type=F32)
-            total = prod + jnp.where(stab[base + 2, k] == 1, acc[...], 0.0)
+        def step(i, carry):
+            total = acc[...]
+            for k in range(8):
+                k += 8 * i
+                tile = V[stab[base, k]]
+                rows = source[stab[base + 1, k]]
+                pair = (tile, rows) if contract else (rows, tile)
+                prod = jnp.dot(*pair, preferred_element_type=F32)
+                total = prod + jnp.where(stab[base + 2, k] == 1, total, 0.0)
+                out[k] = total.astype(out.dtype)
             acc[...] = total
-            out[k] = total.astype(out.dtype)
             return carry
 
-        lax.fori_loop(first, last, step, 0, unroll=4)
+        lax.fori_loop(first // 8, last // 8, step, 0, unroll=1)
 
     def segment(base, segments, j):
         return jnp.where(stab[base + 4, j] == 1, segments[stab[base + 3, j]], 0.0)
@@ -466,7 +470,7 @@
         mine = total2(q, near) + bz[q].astype(F32)
         for k in (0, 1):
             n = 2 * q + k
-            gi[pl.ds(n * T, T), :] = (cscale[n] * mine[k]).astype(BF16)
+            gi[pl.ds(n * T, T), :] = (cscale[n] * jnp.transpose(mine[k])).astype(BF16)
     outs.append(pltpu.make_async_copy(gi, gin_ref, out_sem.at[2]))
     outs[2].start()
 

time: 69.9 us -> 67.3 us (0.963)
  Pallas kernels: 68.6 us -> 65.9 us
    pallas_call x1, Pallas kernels: 66.9 us -> 64.2 us  [body(): pl.pallas_call(kernel, out_shape=outs, in_specs=[anywhere] * 8, out_specs...]
where the time goes in v4:
time: 67.3 us; the launch traced here: 67.2 us
  Pallas kernels  65.9 us (98%)
  between operations  1.29 us (2%)
    pallas_call x1, Pallas kernels, body(): pl.pallas_call(kernel, out_shape=outs, in_specs=[anywhere] * 8, out_specs...  64.2 us
    pallas_call x1, Pallas kernels, body(): pl.pallas_call(leave, out_shape=outs, in_specs=[vmem] * 3, out_specs=(vme...  1.7 us

profile of v4, /device:TPU:1, one launch (start us, length us, event | category | flops | bytes accessed | tf_op | source)
XLA Modules:
  0.0 67.2 jit_solution(16800826483860717592)
XLA Ops:
  1.3 64.2 %shard_map.103 = (bf16[512,128]{1,0:T(8,128)(2,1)}, bf16[512,128]{1,0:T(8,128)(2,1)}, f32[128,128]{1,0:T(8,128)}) custom-call(bf16[512,128]{1,0:T(8,128)(2,1)} %feat.1, bf16[128,128]{1,0:T(8,128)(2,1)} %weight.1, bf16[512,128]{1,0:T(8,128)(2,1)} %cot.1, bf16[128,128,128]{2,1,0:T(8,128)(2,1)} %bitcast.6, s32[2,128]{1,0:T(2,128)} %bitcast.9, ...), custom_call_target="tpu_custom_call" | custom-call | tf_op jit(solution)/shard_map/pallas_call | solution.py:504
  65.5 1.7 %shard_map.104 = (bf16[512,128]{1,0:T(8,128)(2,1)}, bf16[512,128]{1,0:T(8,128)(2,1)}, f32[128,128]{1,0:T(8,128)}) custom-call(bf16[512,128]{1,0:T(8,128)(2,1)} %get-tuple-element.6.refs_0_, bf16[512,128]{1,0:T(8,128)(2,1)} %get-tuple-element.7.refs_1_, f32[128,128]{1,0:T(8,128)} %get-tuple-element.8.refs_2_), custom_call_target="tpu_custom_call" | custom-call | tf_op jit(solution)/shard_map/pallas_call | solution.py:560

commit v5 on v4

--- a/solution.py
+++ b/solution.py
@@ -38,7 +38,7 @@
     cn, X, V, C, G, D, R, Q, F, acc, vtab, stab, cscale, rscale, fe, we, co, rd, cd, lo, gi,
     b1, b2, b3, c1, e1, x1, x2, x3, xc, e2, bz,
     h1, he, u1, u2, u3, uc,
-    w0, a1, a2, a3, a4, s1, full, pad,
+    w0, a1, a2, a3, s1, full, pad,
     load_sem, in_sem, out_sem, tab_sem, send_sem, row_r, sum_r, col_r, fsum_r, ar_r,
 ):
     r, c = lax.axis_index("row"), lax.axis_index("col")
@@ -95,6 +95,7 @@
     friends += [on_x[d] for d in (1, 2, 3)]
     friends += [on_y[d] for d in (1, 2, 3)]
     friends += [on_z(d) for d in range(1, 8)]
+    friends += [(zl * 16 + py[i] * 4 + px[j], c) for i in (1, 2, 3) for j in (1, 2, 3)]
     for friend in friends:
         pl.semaphore_signal(barrier, inc=1, device_id=friend, device_id_type=MESH)
 
@@ -288,8 +289,9 @@
     load.wait()
     table.wait()
     acc[...] = jnp.zeros_like(acc)
-    products(0, 0, 48, G, R, 0)
+    products(0, 0, 24, G, R, 0)
     turn3(far, 3)
+    products(0, 24, 48, G, R, 0)
     turn3(far, 1)
     products(0, 48, 128, G, R, 0)
     turn3(far, 2)
@@ -308,7 +310,7 @@
             src = c1.at[q, zu, o]
         else:
             src = unit(D, q, zu, first[o], second[2] if kind == 0 else along(second, step))
-        i = o if kind == 0 else 4 + o
+        i = 4 * zu + o if kind == 0 else 8 + 4 * zu + o
         send(src, (b1, b2, b3)[kind].at[q, zu, o], send_sem.at[2], sum_r.at[i], device(q, 1, step))
 
     def sum_arrived(i, tiles):
@@ -317,7 +319,7 @@
     def sum_send2(kind, q, zu):
         step = behind_of(zu) if kind == 1 else ahead_of(zu)
         src = (e1.at[q, zu, 2], e1.at[q, zu, step], xc.at[q, zu])[kind]
-        i = 8 if kind == 0 else 9 + zu
+        i = 16 + zu if kind == 0 else 18 + zu
         send(src, (x1, x2, x3)[kind].at[q, zu], send_sem.at[2], sum_r.at[i], device(q, 0, step))
 
     def own_unit(q, zu, o, step):
@@ -326,33 +328,39 @@
 
     order = (2, 1, 3, 0)
     both = [(q, zu) for zu in (far, near) for q in halves]
-    for kind in (0, 1):
-        for o in order:
-            for q, zu in both:
-                sum_send(kind, q, zu, o)
+    for o in order:
+        for q, zu in both:
+            sum_send(0, q, zu, o)
+    for o in order:
+        for q in halves:
+            sum_send(1, q, far, o)
+            sum_send(1, q, near, o)
 
     gathered(13, 32)
 
-    def relay(o):
-        sum_arrived(o, 8)
-        for q, zu in both:
+    def relay(zu, o):
+        sum_arrived(4 * zu + o, 4)
+        for q in halves:
             c1[q, zu, o] = (b1[q, zu, o].astype(F32) + own_unit(q, zu, o, ahead_of(zu))).astype(BF16)
             sum_send(2, q, zu, o)
 
-    def total1(o):
-        sum_arrived(4 + o, 16)
-        for q, zu in both:
+    def total1(zu, o):
+        sum_arrived(8 + 4 * zu + o, 8)
+        for q in halves:
             e1[q, zu, o] = (
                 own_unit(q, zu, o, 0) + b2[q, zu, o].astype(F32) + b3[q, zu, o].astype(F32)
             ).astype(BF16)
 
     acc[...] = jnp.zeros_like(acc)
     products(8, 0, 48, X, Q, 1)
-    relay(2)
+    relay(far, 2)
+    relay(near, 2)
     products(8, 48, 88, X, Q, 1)
-    relay(1)
+    relay(far, 1)
+    relay(near, 1)
     products(8, 88, 128, X, Q, 1)
-    relay(3)
+    relay(far, 3)
+    relay(near, 3)
 
     def scaled(i, carry):
         F[i] = (rscale[i] * segment(8, Q, i)).astype(BF16)
@@ -374,17 +382,12 @@
 
     w0[...] = jnp.zeros_like(w0)
     for owner in range(8):
-
-        def share(k, carry):
-            w0[...] += lax.dot_general(
-                F[4 * owner + k],
-                C[owner, pl.ds(pl.multiple_of(k * T, T), T), :],
-                (((0,), (0,)), ((), ())),
-                preferred_element_type=F32,
-            )
-            return carry
-
-        lax.fori_loop(0, 4, share, 0, unroll=True)
+        w0[...] += lax.dot_general(
+            F[pl.ds(4 * owner, 4)].reshape(512, T),
+            C[owner, pl.ds(0, 512), :],
+            (((0,), (0,)), ((), ())),
+            preferred_element_type=F32,
+        )
 
     def ar_send(i, src, dst, device):
         send(src, dst, send_sem.at[4 if i == 0 else 5], ar_r.at[i], device)
@@ -415,43 +418,52 @@
     for kind in (0, 1):
         for h in halves:
             fsum_send(kind, h)
+    total1(far, 2)
+    for q in halves:
+        sum_send2(0, q, far)
+    relay(far, 0)
     ar_arrived(1, a2)
-    a3[y] = s1[z_rows(0), :] + ((a2[0] + a2[1]) + (a2[2] + a2[3])) + ((a2[4] + a2[5]) + a2[6])
-    for d in (1, 2, 3):
-        ar_send(2, a3.at[y], a3.at[y], on_y[d])
-    total1(2)
-    for q, zu in both:
-        sum_send2(0, q, zu)
-    relay(0)
+    a3[4 * y + x] = s1[z_rows(0), :] + ((a2[0] + a2[1]) + (a2[2] + a2[3])) + ((a2[4] + a2[5]) + a2[6])
+    for i in range(4):
+        for j in range(4):
+            if i or j:
+                ar_send(2, a3.at[4 * y + x], a3.at[4 * y + x], (zl * 16 + py[i] * 4 + px[j], c))
+    total1(far, 1)
+    total1(far, 3)
+    for q in halves:
+        sum_send2(1, q, far)
+    total1(near, 2)
+    for q in halves:
+        sum_send2(0, q, near)
+    relay(near, 0)
     fsum_arrived(2, 4)
     for h in halves:
         step = 1 if h == 0 else 3
         uc[h] = (u1[h].astype(F32) + he[ring(zh, step), pl.ds(2 * h, 2)].astype(F32)).astype(BF16)
         fsum_send(2, h)
-    total1(1)
-    total1(3)
-    for q in halves:
-        sum_send2(1, q, far)
-    ar_arrived(2, a2.at[pl.ds(0, 3)])
-    a4[x] = (a3[0] + a3[1]) + (a3[2] + a3[3])
-    for d in (1, 2, 3):
-        ar_send(3, a4.at[x], a4.at[x], on_x[d])
-    sum_arrived(8, 8)
+    sum_arrived(16 + far, 4)
     for q in halves:
         relay2(q, far)
-    for q in halves:
-        sum_send2(1, q, near)
-    for q in halves:
-        relay2(q, near)
-    total1(0)
-    ar_arrived(3, a2.at[pl.ds(0, 3)])
-    full[z_rows(0), :] = (a4[0] + a4[1]) + (a4[2] + a4[3])
+    ar_arrived(2, a3.at[pl.ds(0, 15)])
+    sums = [a3[i] for i in range(16)]
+    while len(sums) > 1:
+        sums = [sums[i] + sums[i + 1] for i in range(0, len(sums), 2)]
+    full[z_rows(0), :] = sums[0]
     for d in range(1, 8):
         ar_send(4, full.at[z_rows(0)], full.at[z_rows(0)], on_z(d))
-    sum_arrived(9 + far, 8)
+    total1(near, 1)
+    total1(near, 3)
+    for q in halves:
+        sum_send2(1, q, near)
+    sum_arrived(16 + near, 4)
+    for q in halves:
+        relay2(q, near)
+    total1(far, 0)
+    sum_arrived(18 + far, 8)
     for q in halves:
         e2[q] = total2(q, far).astype(BF16)
-        send(e2.at[q], bz.at[q], send_sem.at[2], sum_r.at[11], partner)
+        send(e2.at[q], bz.at[q], send_sem.at[2], sum_r.at[20], partner)
+    total1(near, 0)
 
     fsum_arrived(3, 8)
     for n in range(4):
@@ -464,8 +476,8 @@
     ar_arrived(4, a2)
     outs.append(pltpu.make_async_copy(full, gw_ref, out_sem.at[1]))
     outs[1].start()
-    sum_arrived(9 + near, 8)
-    sum_arrived(11, 4)
+    sum_arrived(18 + near, 8)
+    sum_arrived(20, 4)
     for q in halves:
         mine = total2(q, near) + bz[q].astype(F32)
         for k in (0, 1):
@@ -485,16 +497,22 @@
 
 
 def leave(*refs):
-    n = len(refs) // 2
-    for src, dst in zip(refs[:n], refs[n:]):
-        dst[...] = src[...]
+    sources, results, held, arrive, depart = refs[:3], refs[3:6], refs[6:9], refs[9], refs[10]
+    first = [pltpu.make_async_copy(sources[i], held[i], arrive.at[i]) for i in range(3)]
+    second = [pltpu.make_async_copy(held[i], results[i], depart.at[i]) for i in range(3)]
+    for copy in first:
+        copy.start()
+    for here, there in zip(first, second):
+        here.wait()
+        there.start()
+    for copy in second:
+        copy.wait()
 
 
 def body(features, weight, cotangent, tile_values, tile_coords, tile_count, row_degree, col_degree):
     units = lambda *lead: pltpu.VMEM((*lead, 2, T, T), BF16)
     sems = lambda n: pltpu.SemaphoreType.DMA((n,))
     rows = lambda n: pltpu.VMEM((n, T), F32)
-    vmem = pl.BlockSpec(memory_space=pltpu.VMEM)
     anywhere = pl.BlockSpec(memory_space=pl.ANY)
     outs = (
         jax.ShapeDtypeStruct((512, T), BF16),
@@ -536,13 +554,12 @@
             rows(T),
             rows(T),
             pltpu.VMEM((7, 16, T), F32),
-            pltpu.VMEM((4, 16, T), F32),
-            pltpu.VMEM((4, 16, T), F32),
+            pltpu.VMEM((16, 16, T), F32),
             rows(T),
             rows(T),
-            rows(320),
+            rows(464),
             pltpu.SemaphoreType.DMA, sems(7), sems(3), pltpu.SemaphoreType.DMA,
-            sems(6), sems(14), sems(12), sems(5), sems(4), sems(6),
+            sems(6), sems(14), sems(21), sems(5), sems(4), sems(6),
         ],
         compiler_params=pltpu.CompilerParams(
             collective_id=0, has_side_effects=True, vmem_limit_bytes=60 * 1024 * 1024
@@ -560,8 +577,9 @@
     return pl.pallas_call(
         leave,
         out_shape=outs,
-        in_specs=[vmem] * 3,
-        out_specs=(vmem,) * 3,
+        in_specs=[anywhere] * 3,
+        out_specs=(anywhere,) * 3,
+        scratch_shapes=[*(pltpu.VMEM(out.shape, out.dtype) for out in outs), sems(3), sems(3)],
     )(*results)
 
 

time: 67.3 us -> 67.2 us (level); the launches traced: 67.2 us -> 66.3 us
  Pallas kernels: 65.9 us -> 65 us
    pallas_call x1, Pallas kernels: 64.2 us -> 63.3 us  [body(): pl.pallas_call(kernel, out_shape=outs, in_specs=[anywhere] * 8, out_specs...]
where the time goes in v5:
time: 67.2 us; the launch traced here: 66.3 us
  Pallas kernels  65 us (97%)
  between operations  1.29 us (2%)
    pallas_call x1, Pallas kernels, body(): pl.pallas_call(kernel, out_shape=outs, in_specs=[anywhere] * 8, out_specs...  63.3 us
    pallas_call x1, Pallas kernels, body(): pl.pallas_call(leave, out_shape=outs, in_specs=[anywhere] * 3, out_specs=...  1.69 us

profile of v5, /device:TPU:1, one launch (start us, length us, event | category | flops | bytes accessed | tf_op | source)
XLA Modules:
  0.0 66.3 jit_solution(10583632493776226163)
XLA Ops:
  1.3 63.3 %shard_map.103 = (bf16[512,128]{1,0:T(8,128)(2,1)}, bf16[512,128]{1,0:T(8,128)(2,1)}, f32[128,128]{1,0:T(8,128)}) custom-call(bf16[512,128]{1,0:T(8,128)(2,1)} %feat.1, bf16[128,128]{1,0:T(8,128)(2,1)} %weight.1, bf16[512,128]{1,0:T(8,128)(2,1)} %cot.1, bf16[128,128,128]{2,1,0:T(8,128)(2,1)} %bitcast.6, s32[2,128]{1,0:T(2,128)} %bitcast.9, ...), custom_call_target="tpu_custom_call" | custom-call | tf_op jit(solution)/shard_map/pallas_call | solution.py:522
  64.6 1.7 %shard_map.104 = (bf16[512,128]{1,0:T(8,128)(2,1)}, bf16[512,128]{1,0:T(8,128)(2,1)}, f32[128,128]{1,0:T(8,128)}) custom-call(bf16[512,128]{1,0:T(8,128)(2,1)} %get-tuple-element.6.refs_0_, bf16[512,128]{1,0:T(8,128)(2,1)} %get-tuple-element.7.refs_1_, f32[128,128]{1,0:T(8,128)} %get-tuple-element.8.refs_2_), custom_call_target="tpu_custom_call" | custom-call | tf_op jit(solution)/shard_map/pallas_call | solution.py:577
